TPU v7x, 256 devices: a whole 4x4x8 slice. The times are simulated.
256 devices in a mesh: gx: 4 (over y), gy: 8 (over x, core), gz: 8 (over z).
Axes of the slice: x: 4, y: 4, z: 8, core: 2. Of those that a mesh axis runs over, the one named last changes fastest.
Arguments:
- guess: float32 [64, 256, 1024], P('gx', 'gy', 'gz'), may hold values from -3 to 3
- right_side: float32 [64, 256, 1024], P('gx', 'gy', 'gz'), may hold values from -8 to 8
- screen: float32 [64, 256, 1024], P('gx', 'gy', 'gz'), may hold values from 0.002 to 0.02
Outputs:
- solution: float32 [64, 256, 1024], P('gx', 'gy', 'gz')
All inputs are finite; a program needn't handle non-finite values.
Results may differ from a plain program's by a relative error of at most 0.00011.
Values sent between devices are 32-bit elements; how exact they have to be, the bound alone decides.
A program may use at most 64 MiB of HBM per device.

v0:
```python
import jax
import jax.numpy as jnp
from jax import lax
from jax.sharding import PartitionSpec as P

SWEEPS = 2
ITERS = 16


OMEGA = 0.8
CENTER = 14.0


def padded_2(cells, sides, width):
    for axis, dim in sides:
        count = lax.axis_size(axis)
        ends = count - 1
        head = lax.slice_in_dim(cells, 0, width, axis=dim)
        tail = lax.slice_in_dim(cells, cells.shape[dim] - width, cells.shape[dim], axis=dim)
        cells = jnp.concatenate(
            [
                lax.ppermute(tail, axis, [(i, (i + 1) % count) for i in range(ends)]),
                cells,
                lax.ppermute(head, axis, [((i + 1) % count, i) for i in range(ends)]),
            ],
            axis=dim,
        )
    return cells


def neighbours(padded):
    rows_x = padded.shape[0] - 2
    rows_y = padded.shape[1] - 2
    rows_z = padded.shape[2] - 2
    total = jnp.zeros((rows_x, rows_y, rows_z), jnp.float32)
    for first in range(3):
        for second in range(3):
            for third in range(3):
                count = abs(first - 1) + abs(second - 1) + abs(third - 1)
                if count == 0:
                    continue
                weight = (1.0, 0.5, 0.25)[count - 1]
                total = (
                    total
                    + weight
                    * padded[
                        first : first + rows_x, second : second + rows_y, third : third + rows_z
                    ]
                )
    return total


def misfit(field, padded, rhs, coeff):
    return rhs - ((CENTER + coeff) * field - neighbours(padded))


def relax(field, padded, rhs, coeff):
    return field + OMEGA * misfit(field, padded, rhs, coeff) / (CENTER + coeff)


def restrict(field):
    rows_x, rows_y, rows_z = field.shape
    blocks = field.reshape(rows_x // 2, 2, rows_y // 2, 2, rows_z // 2, 2)
    return 4.0 * jnp.mean(blocks, axis=(1, 3, 5))


def prolong(field):
    return jnp.repeat(jnp.repeat(jnp.repeat(field, 2, axis=0), 2, axis=1), 2, axis=2)


def fine_pad(field):
    return padded_2(field, (("gx", 0), ("gy", 1), ("gz", 2)), 1)


def mid_pad(field):
    return padded_2(field, (("gx", 0), ("gy", 1), ("gz", 2)), 1)


def on_device(guess, right_side, screen):
    fine = guess
    for repeat in range(SWEEPS):
        fine = relax(fine, fine_pad(fine), right_side, screen)
    level_rhs = restrict(misfit(fine, fine_pad(fine), right_side, screen))
    level_coeff = restrict(screen)
    level_corr = OMEGA * level_rhs / (CENTER + level_coeff)
    level_corr = relax(level_corr, mid_pad(level_corr), level_rhs, level_coeff)
    level_misfit = misfit(level_corr, mid_pad(level_corr), level_rhs, level_coeff)
    coarse_rhs = restrict(restrict(level_misfit))
    coarse_coeff = restrict(restrict(level_coeff))

    def brick_step(index, field):
        padded = padded_2(field, (("gx", 0), ("gy", 1), ("gz", 2)), 1)
        return relax(field, padded, coarse_rhs, coarse_coeff)

    coarse_corr = OMEGA * coarse_rhs / (CENTER + coarse_coeff)
    coarse_corr = lax.fori_loop(0, ITERS - 1, brick_step, coarse_corr)
    level_corr = level_corr + prolong(prolong(coarse_corr))
    return fine + prolong(level_corr)


def solution(mesh):
    placed = (P("gx", "gy", "gz"), P("gx", "gy", "gz"), P("gx", "gy", "gz"))
    return jax.shard_map(
        on_device, mesh=mesh, in_specs=placed, out_specs=P("gx", "gy", "gz"), check_vma=False
    )
```

profile of v0, /device:TPU:32, one launch (start us, length us, event | category | flops | bytes accessed | tf_op | source)
XLA Modules:
  0.0 554.5 jit_solution(17546901104785121101)
XLA Ops:
  22.1 6.0 %collective-permute-done.10 = f32[18,34,1]{2,1,0:T(8,128)S(1)} collective-permute-done((f32[18,34,1]{2,1,0:T(8,128)S(1)}, f32[18,34,1]{2,1,0:T(8,128)S(1)}, u32[]{:S(2)}, u32[]{:S(2)}) %collective-permute-start.10) | collective-permute-done | bytes 2480 | tf_op jit(solution)/shard_map/ppermute | solution.py:22
  47.1 4.4 collective-permute-done.15
  51.8 4.8 collective-permute-start.16
  58.6 5.5 collective-permute-done.16
  64.1 5.8 %collective-permute-done.17 = f32[18,34,1]{2,1,0:T(8,128)S(1)} collective-permute-done((f32[18,34,1]{2,1,0:T(8,128)S(1)}, f32[18,34,1]{2,1,0:T(8,128)S(1)}, u32[]{:S(2)}, u32[]{:S(2)}) %collective-permute-start.17) | collective-permute-done | bytes 2480 | tf_op jit(solution)/shard_map/ppermute | solution.py:24
  83.3 18.1 %reshape.49 = f32[8,2,16,2,64,2]{5,4,3,2,1,0:T(8,128)} reshape(f32[16,32,128]{2,1,0:T(8,128)S(1)} %copy-done) | data formatting | bytes 524288 | tf_op jit(solution)/shard_map/reshape | solution.py:63
  101.4 7.0 %reduce_sum.55 = f32[8,16,64]{2,1,0:T(8,128)S(1)} reduce(f32[8,2,16,2,64,2]{5,4,3,2,1,0:T(8,128)} %reshape.49, f32[]{:T(128)} %constant.48.clone.1), dimensions={1,3,5}, to_apply=%region_1.0 | reduce | flops 57344 | bytes 294916 | tf_op jit(solution)/shard_map/reduce_sum | solution.py:64
  114.6 4.8 collective-permute-done.22
  123.7 18.1 %reshape.48 = f32[8,2,16,2,64,2]{5,4,3,2,1,0:T(8,128)} reshape(f32[16,32,128]{2,1,0:T(8,128)S(1)} %fusion.65) | data formatting | bytes 524288 | tf_op jit(solution)/shard_map/reshape | solution.py:63
  141.8 7.0 %reduce_sum.54 = f32[8,16,64]{2,1,0:T(8,128)S(1)} reduce(f32[8,2,16,2,64,2]{5,4,3,2,1,0:T(8,128)} %reshape.48, f32[]{:T(128)} %constant.48.clone.1), dimensions={1,3,5}, to_apply=%region_0.0 | reduce | flops 57344 | bytes 294916 | tf_op jit(solution)/shard_map/reduce_sum | solution.py:64
  161.6 5.6 %collective-permute-done.27 = f32[10,1,64]{2,1,0:T(1,128)S(1)} collective-permute-done((f32[10,1,64]{2,1,0:T(1,128)S(1)}, f32[10,1,64]{2,1,0:T(1,128)S(1)}, u32[]{:S(2)}, u32[]{:S(2)}) %collective-permute-start.27) | collective-permute-done | bytes 2592 | tf_op jit(solution)/shard_map/ppermute | solution.py:24
  206.1 346.2 %while.10 = (s32[]{:T(128)}, f32[2,4,16]{2,1,0:T(4,128)S(1)}, f32[2,4,16]{2,1,0:T(4,128)S(1)}, f32[2,4,16]{2,1,0:T(4,128)S(1)}, s32[]{:T(128)}) while((s32[]{:T(128)}, f32[2,4,16]{2,1,0:T(4,128)S(1)}, f32[2,4,16]{2,1,0:T(4,128)S(1)}, f32[2,4,16]{2,1,0:T(4,128)S(1)}, s32[]{:T(128)}) %tuple.57), condition=%wide.region_7.0_spmd, body=%wide.region_6.0_spmd.sunk | while | flops 10898 | bytes 44589 | solution.py:96
  281.3 4.4 collective-permute-start.3
  304.6 4.4 collective-permute-start.3
  327.9 4.4 collective-permute-start.3
  351.3 4.4 collective-permute-start.3
  374.6 4.4 collective-permute-start.3
  397.9 4.4 collective-permute-start.3
  421.3 4.4 collective-permute-start.3
  444.6 4.4 collective-permute-start.3
  468.0 4.4 collective-permute-start.3
  491.3 4.4 collective-permute-start.3
  514.6 4.4 collective-permute-start.3
  538.0 4.4 collective-permute-start.3
  (442 shorter events, 411.6 us)
Async XLA Ops:
  16.2 11.9 %collective-permute-start.10 = (f32[18,34,1]{2,1,0:T(8,128)S(1)}, f32[18,34,1]{2,1,0:T(8,128)S(1)}, u32[]{:S(2)}, u32[]{:S(2)}) collective-permute-start(f32[18,34,1]{2,1,0:T(8,128)S(1)} %get-tuple-element.48), channel_id=1, source_target_pairs={{0,1},{1,2},{2,3},{3,4},{4,5},{5,6},{6,7},{8,9},{9,10},{10,11},{11... | collective-permute-start | bytes 7352 | tf_op jit(solution)/shard_map/ppermute | solution.py:22
  20.1 12.0 %collective-permute-start.11 = (f32[18,34,1]{2,1,0:T(8,128)S(1)}, f32[18,34,1]{2,1,0:T(8,128)S(1)}, u32[]{:S(2)}, u32[]{:S(2)}) collective-permute-start(f32[18,34,1]{2,1,0:T(8,128)S(1)} %get-tuple-element.49), channel_id=1, source_target_pairs={{1,0},{2,1},{3,2},{4,3},{5,4},{6,5},{7,6},{9,8},{10,9},{11,10},{12... | collective-permute-start | bytes 7352 | tf_op jit(solution)/shard_map/ppermute | solution.py:24
  51.8 12.3 %collective-permute-start.16 = (f32[18,34,1]{2,1,0:T(8,128)S(1)}, f32[18,34,1]{2,1,0:T(8,128)S(1)}, u32[]{:S(2)}, u32[]{:S(2)}) collective-permute-start(f32[18,34,1]{2,1,0:T(8,128)S(1)} %get-tuple-element.46), channel_id=1, source_target_pairs={{0,1},{1,2},{2,3},{3,4},{4,5},{5,6},{6,7},{8,9},{9,10},{10,11},{11... | collective-permute-start | bytes 7352 | tf_op jit(solution)/shard_map/ppermute | solution.py:22
  56.7 13.3 %collective-permute-start.17 = (f32[18,34,1]{2,1,0:T(8,128)S(1)}, f32[18,34,1]{2,1,0:T(8,128)S(1)}, u32[]{:S(2)}, u32[]{:S(2)}) collective-permute-start(f32[18,34,1]{2,1,0:T(8,128)S(1)} %get-tuple-element.47), channel_id=1, source_target_pairs={{1,0},{2,1},{3,2},{4,3},{5,4},{6,5},{7,6},{9,8},{10,9},{11,10},{12... | collective-permute-start | bytes 7352 | tf_op jit(solution)/shard_map/ppermute | solution.py:24
  80.0 28.4 %collective-permute-start.20 = (f32[18,1,128]{2,1,0:T(1,128)S(1)}, f32[18,1,128]{2,1,0:T(1,128)S(1)}, u32[]{:S(2)}, u32[]{:S(2)}) collective-permute-start(f32[18,1,128]{2,1,0:T(1,128)S(1)} %get-tuple-element.58), channel_id=1, source_target_pairs={{0,8},{8,16},{16,24},{24,32},{32,40},{40,48},{48,56},{1,9},{9,17},... | collective-permute-start | bytes 27656 | tf_op jit(solution)/shard_map/ppermute | solution.py:22
  82.0 26.4 %collective-permute-start.21 = (f32[18,1,128]{2,1,0:T(1,128)S(1)}, f32[18,1,128]{2,1,0:T(1,128)S(1)}, u32[]{:S(2)}, u32[]{:S(2)}) collective-permute-start(f32[18,1,128]{2,1,0:T(1,128)S(1)} %get-tuple-element.59), channel_id=1, source_target_pairs={{8,0},{16,8},{24,16},{32,24},{40,32},{48,40},{56,48},{9,1},{17,9},... | collective-permute-start | bytes 27656 | tf_op jit(solution)/shard_map/ppermute | solution.py:24
  108.7 10.8 %collective-permute-start.22 = (f32[18,34,1]{2,1,0:T(8,128)S(1)}, f32[18,34,1]{2,1,0:T(8,128)S(1)}, u32[]{:S(2)}, u32[]{:S(2)}) collective-permute-start(f32[18,34,1]{2,1,0:T(8,128)S(1)} %get-tuple-element.44), channel_id=1, source_target_pairs={{0,1},{1,2},{2,3},{3,4},{4,5},{5,6},{6,7},{8,9},{9,10},{10,11},{11... | collective-permute-start | bytes 7352 | tf_op jit(solution)/shard_map/ppermute | solution.py:22
  112.3 10.4 %collective-permute-start.23 = (f32[18,34,1]{2,1,0:T(8,128)S(1)}, f32[18,34,1]{2,1,0:T(8,128)S(1)}, u32[]{:S(2)}, u32[]{:S(2)}) collective-permute-start(f32[18,34,1]{2,1,0:T(8,128)S(1)} %get-tuple-element.45), channel_id=1, source_target_pairs={{1,0},{2,1},{3,2},{4,3},{5,4},{6,5},{7,6},{9,8},{10,9},{11,10},{12... | collective-permute-start | bytes 7352 | tf_op jit(solution)/shard_map/ppermute | solution.py:24
  160.3 6.9 %collective-permute-start.27 = (f32[10,1,64]{2,1,0:T(1,128)S(1)}, f32[10,1,64]{2,1,0:T(1,128)S(1)}, u32[]{:S(2)}, u32[]{:S(2)}) collective-permute-start(f32[10,1,64]{2,1,0:T(1,128)S(1)} %get-tuple-element.87), channel_id=1, source_target_pairs={{8,0},{16,8},{24,16},{32,24},{40,32},{48,40},{56,48},{9,1},{17,9},... | collective-permute-start | bytes 7688 | tf_op jit(solution)/shard_map/ppermute | solution.py:24
  167.3 6.8 %collective-permute-start.28 = (f32[10,18,1]{2,1,0:T(8,128)S(1)}, f32[10,18,1]{2,1,0:T(8,128)S(1)}, u32[]{:S(2)}, u32[]{:S(2)}) collective-permute-start(f32[10,18,1]{2,1,0:T(8,128)S(1)} %get-tuple-element.74), channel_id=1, source_target_pairs={{0,1},{1,2},{2,3},{3,4},{4,5},{5,6},{6,7},{8,9},{9,10},{10,11},{11... | collective-permute-start | bytes 2168 | tf_op jit(solution)/shard_map/ppermute | solution.py:22
  170.3 6.9 %collective-permute-start.29 = (f32[10,18,1]{2,1,0:T(8,128)S(1)}, f32[10,18,1]{2,1,0:T(8,128)S(1)}, u32[]{:S(2)}, u32[]{:S(2)}) collective-permute-start(f32[10,18,1]{2,1,0:T(8,128)S(1)} %get-tuple-element.75), channel_id=1, source_target_pairs={{1,0},{2,1},{3,2},{4,3},{5,4},{6,5},{7,6},{9,8},{10,9},{11,10},{12... | collective-permute-start | bytes 2168 | tf_op jit(solution)/shard_map/ppermute | solution.py:24
  192.6 6.8 %collective-permute-start.34 = (f32[10,18,1]{2,1,0:T(8,128)S(1)}, f32[10,18,1]{2,1,0:T(8,128)S(1)}, u32[]{:S(2)}, u32[]{:S(2)}) collective-permute-start(f32[10,18,1]{2,1,0:T(8,128)S(1)} %get-tuple-element.72), channel_id=1, source_target_pairs={{0,1},{1,2},{2,3},{3,4},{4,5},{5,6},{6,7},{8,9},{9,10},{10,11},{11... | collective-permute-start | bytes 2168 | tf_op jit(solution)/shard_map/ppermute | solution.py:22
  196.0 6.9 %collective-permute-start.35 = (f32[10,18,1]{2,1,0:T(8,128)S(1)}, f32[10,18,1]{2,1,0:T(8,128)S(1)}, u32[]{:S(2)}, u32[]{:S(2)}) collective-permute-start(f32[10,18,1]{2,1,0:T(8,128)S(1)} %get-tuple-element.73), channel_id=1, source_target_pairs={{1,0},{2,1},{3,2},{4,3},{5,4},{6,5},{7,6},{9,8},{10,9},{11,10},{12... | collective-permute-start | bytes 2168 | tf_op jit(solution)/shard_map/ppermute | solution.py:24
  219.7 5.8 %collective-permute-start.4 = (f32[4,6,1]{2,1,0:T(8,128)S(1)}, f32[4,6,1]{2,1,0:T(8,128)S(1)}, u32[]{:S(2)}, u32[]{:S(2)}) collective-permute-start(f32[4,6,1]{2,1,0:T(8,128)S(1)} %get-tuple-element.134), channel_id=1, source_target_pairs={{0,1},{1,2},{2,3},{3,4},{4,5},{5,6},{6,7},{8,9},{9,10},{10,11},{11... | collective-permute-start | bytes 296 | tf_op jit(solution)/shard_map/while/body/eval_jaxpr/ppermute | solution.py:22
  241.7 5.8 %collective-permute-start.4 = (f32[4,6,1]{2,1,0:T(8,128)S(1)}, f32[4,6,1]{2,1,0:T(8,128)S(1)}, u32[]{:S(2)}, u32[]{:S(2)}) collective-permute-start(f32[4,6,1]{2,1,0:T(8,128)S(1)} %get-tuple-element.134), channel_id=1, source_target_pairs={{0,1},{1,2},{2,3},{3,4},{4,5},{5,6},{6,7},{8,9},{9,10},{10,11},{11... | collective-permute-start | bytes 296 | tf_op jit(solution)/shard_map/while/body/eval_jaxpr/ppermute | solution.py:22
  263.3 5.8 %collective-permute-start.4 = (f32[4,6,1]{2,1,0:T(8,128)S(1)}, f32[4,6,1]{2,1,0:T(8,128)S(1)}, u32[]{:S(2)}, u32[]{:S(2)}) collective-permute-start(f32[4,6,1]{2,1,0:T(8,128)S(1)} %get-tuple-element.134), channel_id=1, source_target_pairs={{0,1},{1,2},{2,3},{3,4},{4,5},{5,6},{6,7},{8,9},{9,10},{10,11},{11... | collective-permute-start | bytes 296 | tf_op jit(solution)/shard_map/while/body/eval_jaxpr/ppermute | solution.py:22
  286.6 5.8 %collective-permute-start.4 = (f32[4,6,1]{2,1,0:T(8,128)S(1)}, f32[4,6,1]{2,1,0:T(8,128)S(1)}, u32[]{:S(2)}, u32[]{:S(2)}) collective-permute-start(f32[4,6,1]{2,1,0:T(8,128)S(1)} %get-tuple-element.134), channel_id=1, source_target_pairs={{0,1},{1,2},{2,3},{3,4},{4,5},{5,6},{6,7},{8,9},{9,10},{10,11},{11... | collective-permute-start | bytes 296 | tf_op jit(solution)/shard_map/while/body/eval_jaxpr/ppermute | solution.py:22
  310.0 5.8 %collective-permute-start.4 = (f32[4,6,1]{2,1,0:T(8,128)S(1)}, f32[4,6,1]{2,1,0:T(8,128)S(1)}, u32[]{:S(2)}, u32[]{:S(2)}) collective-permute-start(f32[4,6,1]{2,1,0:T(8,128)S(1)} %get-tuple-element.134), channel_id=1, source_target_pairs={{0,1},{1,2},{2,3},{3,4},{4,5},{5,6},{6,7},{8,9},{9,10},{10,11},{11... | collective-permute-start | bytes 296 | tf_op jit(solution)/shard_map/while/body/eval_jaxpr/ppermute | solution.py:22
  333.3 5.8 %collective-permute-start.4 = (f32[4,6,1]{2,1,0:T(8,128)S(1)}, f32[4,6,1]{2,1,0:T(8,128)S(1)}, u32[]{:S(2)}, u32[]{:S(2)}) collective-permute-start(f32[4,6,1]{2,1,0:T(8,128)S(1)} %get-tuple-element.134), channel_id=1, source_target_pairs={{0,1},{1,2},{2,3},{3,4},{4,5},{5,6},{6,7},{8,9},{9,10},{10,11},{11... | collective-permute-start | bytes 296 | tf_op jit(solution)/shard_map/while/body/eval_jaxpr/ppermute | solution.py:22
  356.6 5.8 %collective-permute-start.4 = (f32[4,6,1]{2,1,0:T(8,128)S(1)}, f32[4,6,1]{2,1,0:T(8,128)S(1)}, u32[]{:S(2)}, u32[]{:S(2)}) collective-permute-start(f32[4,6,1]{2,1,0:T(8,128)S(1)} %get-tuple-element.134), channel_id=1, source_target_pairs={{0,1},{1,2},{2,3},{3,4},{4,5},{5,6},{6,7},{8,9},{9,10},{10,11},{11... | collective-permute-start | bytes 296 | tf_op jit(solution)/shard_map/while/body/eval_jaxpr/ppermute | solution.py:22
  380.0 5.8 %collective-permute-start.4 = (f32[4,6,1]{2,1,0:T(8,128)S(1)}, f32[4,6,1]{2,1,0:T(8,128)S(1)}, u32[]{:S(2)}, u32[]{:S(2)}) collective-permute-start(f32[4,6,1]{2,1,0:T(8,128)S(1)} %get-tuple-element.134), channel_id=1, source_target_pairs={{0,1},{1,2},{2,3},{3,4},{4,5},{5,6},{6,7},{8,9},{9,10},{10,11},{11... | collective-permute-start | bytes 296 | tf_op jit(solution)/shard_map/while/body/eval_jaxpr/ppermute | solution.py:22
  403.3 5.8 %collective-permute-start.4 = (f32[4,6,1]{2,1,0:T(8,128)S(1)}, f32[4,6,1]{2,1,0:T(8,128)S(1)}, u32[]{:S(2)}, u32[]{:S(2)}) collective-permute-start(f32[4,6,1]{2,1,0:T(8,128)S(1)} %get-tuple-element.134), channel_id=1, source_target_pairs={{0,1},{1,2},{2,3},{3,4},{4,5},{5,6},{6,7},{8,9},{9,10},{10,11},{11... | collective-permute-start | bytes 296 | tf_op jit(solution)/shard_map/while/body/eval_jaxpr/ppermute | solution.py:22
  426.6 5.8 %collective-permute-start.4 = (f32[4,6,1]{2,1,0:T(8,128)S(1)}, f32[4,6,1]{2,1,0:T(8,128)S(1)}, u32[]{:S(2)}, u32[]{:S(2)}) collective-permute-start(f32[4,6,1]{2,1,0:T(8,128)S(1)} %get-tuple-element.134), channel_id=1, source_target_pairs={{0,1},{1,2},{2,3},{3,4},{4,5},{5,6},{6,7},{8,9},{9,10},{10,11},{11... | collective-permute-start | bytes 296 | tf_op jit(solution)/shard_map/while/body/eval_jaxpr/ppermute | solution.py:22
  450.0 5.8 %collective-permute-start.4 = (f32[4,6,1]{2,1,0:T(8,128)S(1)}, f32[4,6,1]{2,1,0:T(8,128)S(1)}, u32[]{:S(2)}, u32[]{:S(2)}) collective-permute-start(f32[4,6,1]{2,1,0:T(8,128)S(1)} %get-tuple-element.134), channel_id=1, source_target_pairs={{0,1},{1,2},{2,3},{3,4},{4,5},{5,6},{6,7},{8,9},{9,10},{10,11},{11... | collective-permute-start | bytes 296 | tf_op jit(solution)/shard_map/while/body/eval_jaxpr/ppermute | solution.py:22
  (98 other events, 622.6 us)
where the time goes:
time: 564 us; the launch traced here: 554 us
  starting transfers between devices  290 us (51%)
  waiting for transfers between devices  192 us (34%)
  local copies, waits for them, and re-layouts  46.2 us (8%)
  other arithmetic  24.4 us (4%)
    ppermute x60, starting transfers between devices, padded_2(): lax.ppermute(tail, axis, [(i, (i + 1) % count) for i in range(ends)])  186 us
    ppermute x60, waiting for transfers between devices, padded_2(): lax.ppermute(head, axis, [((i + 1) % count, i) for i in range(ends)])  161 us
    ppermute x60, starting transfers between devices, padded_2(): lax.ppermute(head, axis, [((i + 1) % count, i) for i in range(ends)])  104 us
    reshape x3, local copies, waits for them, and re-layouts, restrict(): blocks = field.reshape(rows_x // 2, 2, rows_y // 2, 2, rows_z // 2, 2)  38.3 us
    ppermute x60, waiting for transfers between devices, padded_2(): lax.ppermute(tail, axis, [(i, (i + 1) % count) for i in range(ends)])  30.4 us
    reduce_sum x6, other arithmetic, restrict(): return 4.0 * jnp.mean(blocks, axis=(1, 3, 5))  14.6 us
  transfers between devices with their start and end apart: 120, of which 67 were waited for; matrix products, arithmetic and copies ran while one was open for 5% of the time, Pallas kernels for 0%

commit v1 on v0

v1 whole, which is shorter than its diff:
```python
import functools
import itertools

import jax
import jax.numpy as jnp
from jax import lax
from jax.experimental import pallas as pl
from jax.experimental.pallas import tpu as pltpu
from jax.sharding import PartitionSpec as P

ITERS = 16
OMEGA = 0.8
CENTER = 14.0
F32 = jnp.float32
MESH = pl.DeviceIdType.MESH
HIGH = lax.Precision.HIGHEST

NX, NY, NZ = 16, 32, 128
PX, PY, PZ = 22, 40, 256
NEIGHBOURS = sorted(
    (o for o in itertools.product((-1, 0, 1), repeat=3) if o != (0, 0, 0)),
    key=lambda o: (-sum(abs(v) for v in o)),
)


def iota(shape, dim):
    return lax.broadcasted_iota(jnp.int32, shape, dim)


def mod(v, n):
    return lax.rem(v + n, n)


def plane_sum(v):
    rows, cols = v.shape
    a = v + v + pltpu.roll(v, 1, 1) + pltpu.roll(v, cols - 1, 1)
    return a + a + pltpu.roll(a, 1, 0) + pltpu.roll(a, rows - 1, 0)


def kernel(
    sizes,
    guess,
    rhs,
    scr,
    out,
    mm,
    cc,
    va,
    vb,
    packs,
    zland,
    rx,
    sx,
    s24,
    c1r,
    s1r,
    ex,
    zpack,
    zmid,
    e1f,
    msg,
    cmsg,
    bf,
    bc,
    cof,
    coc,
    cov,
    eout,
    dummy_f,
    dummy_c,
    load_sem,
    fs,
    fr,
    ms,
    mr,
    gsem,
):
    gx, gy, gz = sizes
    ix, iy, iz = lax.axis_index("gx"), lax.axis_index("gy"), lax.axis_index("gz")

    def device(o):
        return (
            ix if o[0] == 0 else lax.rem(ix + o[0] % gx, gx),
            iy if o[1] == 0 else lax.rem(iy + o[1] % gy, gy),
            iz if o[2] == 0 else lax.rem(iz + o[2] % gz, gz),
        )

    peers = [
        o
        for o in itertools.product(range(gx), range(gy), (-1, 0, 1))
        if o != (0, 0, 0)
    ]
    peers = [(a - gx if a > gx // 2 else a, b - gy if b > gy // 2 else b, c) for a, b, c in peers]
    peers.sort(key=lambda o: -(abs(o[0]) + (abs(o[1]) + 1) // 2 + abs(o[2])))

    own = []
    for a, ref in enumerate((scr, rhs, guess)):
        copy = pltpu.make_async_copy(ref, mm.at[2 - a, pl.ds(3, NX), pl.ds(0, NY), pl.ds(0, NZ)], load_sem.at[a])
        copy.start()
        own.append(copy)
    for a in range(3):
        for p in range(PX):
            mm[a, p, NY:PY, 0:NZ] = jnp.zeros((PY - NY, NZ), F32)
    for side in range(2):
        for xs in range(3):
            zland[side, xs, NY:PY, :] = jnp.zeros((PY - NY, 128), F32)
            zmid[side, xs, 16:24, :] = jnp.zeros((8, 128), F32)
    ex[...] = jnp.zeros_like(ex)
    s24[...] = jnp.zeros_like(s24)

    barrier = pltpu.get_barrier_semaphore()
    for o in peers:
        pl.semaphore_signal(barrier, inc=1, device_id=device(o), device_id_type=MESH)

    r_i, c_i = iota((128, 128), 0), iota((128, 128), 1)
    pool = jnp.where(r_i // 2 == c_i, 0.5, 0.0).astype(F32)
    pool_halo = jnp.where(
        ((r_i < 2) & (c_i == 64)) | ((r_i >= 126) & (c_i == 127)), 0.5, 0.0
    ).astype(F32)
    copy_mid = jnp.where((c_i // 2 == r_i), 1.0, 0.0).astype(F32)
    copy_coarse = jnp.where((c_i // 8 == r_i), 1.0, 0.0).astype(F32)
    z_of = jnp.where(r_i < 64, r_i // 4 + 1, jnp.where(r_i < 68, 17, jnp.where(r_i >= 124, 0, 99)))
    gather_f = jnp.where((c_i % 20 == z_of) & (c_i < 120), 0.25, 0.0).astype(F32)
    gather_c = jnp.where((r_i // 4 == c_i % 16) & (r_i < 64), 0.25, 0.0).astype(F32)

    def dot(a, b):
        return jnp.dot(a, b, precision=HIGH, preferred_element_type=F32)

    for copy in own:
        copy.wait()

    for q in range(8):
        rx[q] = mm[2, 3 + 2 * q, 0:NY, 0:NZ] + mm[2, 4 + 2 * q, 0:NY, 0:NZ]
    s1_own = dot((rx[:, pl.ds(0, 16, 2), :] + rx[:, pl.ds(1, 16, 2), :]).reshape(128, 128), pool).reshape(8, 16, 128)
    lanes16 = iota((16, 128), 1)
    rows16 = iota((16, 128), 0)
    for xc in range(2):
        s4 = s1_own[4 * xc] + s1_own[4 * xc + 1] + s1_own[4 * xc + 2] + s1_own[4 * xc + 3]
        s4 = dot(s4, gather_c)
        s3 = jnp.sum(jnp.where((lanes16 // 16) % 4 == rows16 // 4, s4, 0.0), axis=0, keepdims=True)
        c3 = OMEGA / (CENTER + s3)
        for k in range(3):
            cmsg[k, xc : xc + 1, :] = c3 if k == 0 else pltpu.roll(c3, 16 * k, 1)

    lane = iota((NY, 128), 1)
    head = jnp.zeros((NY, 128), F32)
    tail = jnp.zeros((NY, 128), F32)
    for p in range(NX):
        g = mm[0, 3 + p, 0:NY, 0:NZ]
        f = mm[1, 3 + p, 0:NY, 0:NZ]
        s = mm[2, 3 + p, 0:NY, 0:NZ]

        def put(acc, v, to, at, count):
            first = 8 * p + to
            return jnp.where((lane >= first) & (lane < first + count), pltpu.roll(v, (first - at) % 128, 1), acc)

        head = put(head, g, 0, 0, 3)
        head = put(head, f, 3, 0, 2)
        head = put(head, s, 5, 0, 2)
        tail = put(tail, g, 5, 125, 3)
        tail = put(tail, f, 3, 126, 2)
        tail = put(tail, s, 1, 126, 2)
    packs[0] = head
    packs[1] = tail

    pl.semaphore_wait(barrier, len(peers))

    fine_copies = []

    def send_fine(o, src, dst):
        i = len(fine_copies)
        copy = pltpu.make_async_remote_copy(
            src_ref=src, dst_ref=dst, send_sem=fs.at[i], recv_sem=fr.at[i], device_id=device(o), device_id_type=MESH
        )
        copy.start()
        fine_copies.append(copy)

    def x_part(d, depth):
        if d == 0:
            return (3, NX), (3, NX)
        return ((3 + NX - depth, depth), (3 - depth, depth)) if d == 1 else ((3, depth), (3 + NX, depth))

    def y_part(d, depth):
        if d == 0:
            return (0, NY), (0, NY)
        return ((NY - depth, depth), (PY - depth, depth)) if d == 1 else ((0, depth), (NY, depth))

    for o in ((1, 0, 0), (-1, 0, 0)):
        for a, depth in ((0, 3), (1, 2), (2, 2)):
            (p0, n), (q0, _) = x_part(o[0], depth)
            send_fine(
                o,
                mm.at[a, pl.ds(p0, n), pl.ds(0, NY), pl.ds(0, NZ)],
                mm.at[a, pl.ds(q0, n), pl.ds(0, NY), pl.ds(0, NZ)],
            )
    for o in NEIGHBOURS:
        dx, dy, dz = o
        (s0, sn), (t0, _) = y_part(dy, 3)
        if dz == 0:
            if dy == 0:
                continue
            (p0, n), (q0, _) = x_part(dx, 3)
            send_fine(
                o,
                mm.at[:, pl.ds(p0, n), pl.ds(s0, sn), pl.ds(0, NZ)],
                mm.at[:, pl.ds(q0, n), pl.ds(t0, sn), pl.ds(0, NZ)],
            )
        else:
            side = 1 if dz == 1 else 0
            send_fine(o, packs.at[side, pl.ds(s0, sn), :], zland.at[side, 1 - dx, pl.ds(t0, sn), :])

    c_copies = []
    for o in peers:
        copy = pltpu.make_async_remote_copy(
            src_ref=cmsg.at[1 - o[2]],
            dst_ref=bc.at[1 - o[2], iy, pl.ds(2 * ix, 2), :],
            send_sem=gsem.at[0],
            recv_sem=gsem.at[1],
            device_id=device(o),
            device_id_type=MESH,
        )
        copy.start()
        c_copies.append(copy)
    pltpu.make_async_copy(cmsg.at[1], bc.at[1, iy, pl.ds(2 * ix, 2), :], gsem.at[1]).start()

    for copy in fine_copies:
        copy.wait_recv()

    rows_in = iota((PY, 128), 0)
    lane40 = iota((PY, 128), 1)
    row_ok = ((rows_in < 36) | (iy > 0)) & ((rows_in < NY) | (rows_in >= 36) | (iy < gy - 1))
    col_ok = ((lane40 < 64) & (iz < gz - 1)) | ((lane40 >= 64) & (iz > 0))
    both_ok = row_ok & col_ok
    for p in range(PX):
        if p < 3:
            xs, q, x_ok = 0, NX - 3 + p, ix > 0
        elif p < 3 + NX:
            xs, q, x_ok = 1, p - 3, None
        else:
            xs, q, x_ok = 2, p - 3 - NX, ix < gx - 1
        h = zland[0, xs]
        t = zland[1, xs]
        ok0 = row_ok if x_ok is None else row_ok & x_ok
        ok1 = both_ok if x_ok is None else both_ok & x_ok
        g1 = jnp.where(
            lane40 < 64, pltpu.roll(h, (-8 * q) % 128, 1), pltpu.roll(t, (-8 * q - 8) % 128, 1)
        )
        mm[0, p, :, NZ:PZ] = jnp.where(ok1, g1, 0.0)
        if x_ok is None:
            mm[0, p, NY:PY, 0:NZ] = jnp.where(ok0[NY:PY], mm[0, p, NY:PY, 0:NZ], 0.0)
        else:
            mm[0, p, :, 0:NZ] = jnp.where(ok0, mm[0, p, :, 0:NZ], 0.0)
        if 0 < p < PX - 1:
            f1 = jnp.where(lane40 < 64, pltpu.roll(h, (-8 * q - 3) % 128, 1), pltpu.roll(t, (-8 * q - 5) % 128, 1))
            s1 = jnp.where(lane40 < 64, pltpu.roll(h, (-8 * q - 5) % 128, 1), pltpu.roll(t, (-8 * q - 3) % 128, 1))
            s1 = jnp.where((lane40 < 2) | (lane40 >= 126), s1, 0.0)
            mm[1, p, :, NZ:PZ] = f1
            mm[2, p, :, NZ:PZ] = s1
            cc[p, :, 0:NZ] = jnp.where(ok0, OMEGA / (CENTER + mm[2, p, :, 0:NZ]), 0.0)
            cc[p, :, NZ:PZ] = jnp.where(ok1, OMEGA / (CENTER + s1), 0.0)

    def sweep(src, dst, first, last):
        def body(p, carry):
            b0, b1 = carry
            b2 = plane_sum(src[p + 1])
            v = src[p]
            t = b0 + b1 + b1 + b2
            dst[p] = 0.2 * v + cc[p] * (mm[1, p] + 0.25 * t - 2.0 * v)
            return b1, b2

        lax.fori_loop(first, last, body, (plane_sum(src[first - 1]), plane_sum(src[first])), unroll=2)

    sweep(mm.at[0], va, 1, PX - 1)
    sweep(va, vb, 2, PX - 2)

    def residual(p, b0, b1):
        b2 = plane_sum(vb[p + 1])[0:NY, 0:NZ]
        t = b0 + b1 + b1 + b2
        v = vb[p, 0:NY, 0:NZ]
        return mm[1, p, 0:NY, 0:NZ] - (CENTER + 2.0 + mm[2, p, 0:NY, 0:NZ]) * v + 0.25 * t, b2

    def pair(q, carry):
        b0, b1 = carry
        r0, b2 = residual(3 + 2 * q, b0, b1)
        r1, b3 = residual(4 + 2 * q, b1, b2)
        rx[q] = r0 + r1
        return b2, b3

    lax.fori_loop(0, 8, pair, (plane_sum(vb[2])[0:NY, 0:NZ], plane_sum(vb[3])[0:NY, 0:NZ]))
    f1 = dot((rx[:, pl.ds(0, 16, 2), :] + rx[:, pl.ds(1, 16, 2), :]).reshape(128, 128), pool).reshape(8, 16, 128)

    for q in range(10):
        sx[0, q] = mm[2, 1 + 2 * q, :, 0:NZ] + mm[2, 2 + 2 * q, :, 0:NZ]
        sx[1, q] = mm[2, 1 + 2 * q, :, NZ:PZ] + mm[2, 2 + 2 * q, :, NZ:PZ]
    for half in range(2):
        v = sx[half, :, pl.ds(0, 20, 2), :] + sx[half, :, pl.ds(1, 20, 2), :]
        s24[half, :, 0:20, :] = v
        s24[half, :, 23:24, :] = v[:, 19:20, :]
    s1 = dot(s24[0].reshape(240, 128), pool) + dot(s24[1].reshape(240, 128), pool_halo)
    s1 = s1.reshape(10, 24, 128)
    row24, lane24 = iota((24, 128), 0), iota((24, 128), 1)
    ok24 = (
        ((row24 < 20) | (iy > 0))
        & ((row24 < 16) | (row24 >= 20) | (iy < gy - 1))
        & ((lane24 < 96) | (iz > 0))
        & ((lane24 < 64) | (lane24 >= 96) | (iz < gz - 1))
    )
    for q in range(10):
        ok = ok24 & (ix > 0) if q == 0 else (ok24 & (ix < gx - 1) if q == 9 else ok24)
        s1r[q] = s1[q]
        c1r[q] = jnp.where(ok, OMEGA / (CENTER + s1[q]), 0.0)

    zero8 = jnp.zeros((8, 128), F32)
    f1z = [jnp.concatenate([f1[q], zero8], axis=0) for q in range(8)]
    e_own = [c1r[q + 1] * f1z[q] for q in range(8)]
    for q in range(8):
        ex[q + 1, 0:16, :] = e_own[q][0:16]

    def weigh(b, p):
        terms = [b[i] * w for i, w in ((p - 1, 1.0), (p, 2.0), (p + 1, 1.0)) if i in b]
        return 0.25 * functools.reduce(lambda m, n: m + n, terms)

    sums = {q: plane_sum(e_own[q]) for q in range(8)}
    e_two = {}
    for q in range(-1, 9):
        t = weigh(sums, q)
        if 0 <= q < 8:
            e_two[q] = 0.2 * e_own[q] + c1r[q + 1] * (f1z[q] + t - 2.0 * e_own[q])
        else:
            e_two[q] = c1r[q + 1] * t
    sums = {q: plane_sum(e_two[q]) for q in range(-1, 9)}
    parts = {}
    for q in range(-2, 10):
        r = weigh(sums, q)
        if q in e_two:
            r = r - (CENTER + 2.0 + s1r[q + 1]) * e_two[q]
        if 0 <= q < 8:
            r = r + f1z[q]
        at = (q + 4) // 4
        parts[at] = parts[at] + r if at in parts else r
    y_of = jnp.where(row24 < 16, row24 // 4 + 1, jnp.where(row24 < 18, 5, jnp.where(row24 >= 22, 0, 99)))
    z_at = lane24 % 20
    keep = (lane24 // 20 == y_of) & ((z_at != 0) | (iz > 0)) & ((z_at != 17) | (iz < gz - 1))
    stacked = dot(jnp.concatenate([parts[i] for i in range(4)], axis=0), gather_f)
    for i in range(4):
        row = jnp.sum(jnp.where(keep, stacked[24 * i : 24 * i + 24], 0.0), axis=0, keepdims=True)
        for k in range(3):
            msg[k, i : i + 1, :] = row if k == 0 else pltpu.roll(row, 16 * k, 1)

    slot = bf.at[:, lax.rem(ix, 2), iy, pl.ds(4 * (ix // 2), 4), :]
    for o in peers:
        copy = pltpu.make_async_remote_copy(
            src_ref=msg.at[1 - o[2]],
            dst_ref=slot.at[1 - o[2]],
            send_sem=gsem.at[2],
            recv_sem=gsem.at[3],
            device_id=device(o),
            device_id_type=MESH,
        )
        copy.start()
    pltpu.make_async_copy(msg.at[1], slot.at[1], gsem.at[3]).start()

    ztail = jnp.zeros((16, 128), F32)
    for q in range(8):
        ztail = jnp.where(lanes16 == q, pltpu.roll(e_own[q][0:16], (q - 63) % 128, 1), ztail)
        ztail = jnp.where(lanes16 == 64 + q, pltpu.roll(e_own[q][0:16], 64 + q, 1), ztail)
    zpack[...] = ztail
    mid_copies = []
    for o in NEIGHBOURS:
        dx, dy, dz = o
        (s0, sn), t0 = ((0, 16), 0) if dy == 0 else (((15, 1), 23) if dy == 1 else ((0, 1), 16))
        if dz == 0:
            (p0, n), q0 = ((1, 8), 1) if dx == 0 else (((8, 1), 0) if dx == 1 else ((1, 1), 9))
            src = ex.at[pl.ds(p0, n), pl.ds(s0, sn), :]
            dst = ex.at[pl.ds(q0, n), pl.ds(t0, sn), :]
        else:
            side = 1 if dz == 1 else 0
            src = zpack.at[pl.ds(s0, sn), :]
            dst = zmid.at[side, 1 - dx, pl.ds(t0, sn), :]
        i = len(mid_copies)
        copy = pltpu.make_async_remote_copy(
            src_ref=src, dst_ref=dst, send_sem=ms.at[i], recv_sem=mr.at[i], device_id=device(o), device_id_type=MESH
        )
        copy.start()
        mid_copies.append(copy)

    pltpu.make_async_copy(bc, bc, gsem.at[1]).wait()
    lane8, row8 = iota((8, 128), 1), iota((8, 128), 0)
    block = (lane8 // 16) % 4
    z_ok = (block < 3) & ((block > 0) | (iz > 0)) & ((block < 2) | (iz < gz - 1))
    low = lane8 < 64
    half = {}
    for y in range(32):
        j, yy = y // 4, y % 4
        d = (lane8 // 16 - yy + 8) % 4
        v = jnp.where(d == 0, bc[0, j], jnp.where(d == 1, bc[1, j], bc[2, j]))
        if yy:
            v = pltpu.roll(v, 128 - 16 * yy, 1)
        if y < 16:
            half[y] = v
        else:
            coc[y - 16] = jnp.where(z_ok, jnp.where(low, half[y - 16], v), 0.0)

    for copy in mid_copies:
        copy.wait_recv()
    mid_sums = {}
    for p in range(10):
        if p == 0:
            xs, q, x_ok = 0, 7, ix > 0
        elif p < 9:
            xs, q, x_ok = 1, p - 1, None
        else:
            xs, q, x_ok = 2, 0, ix < gx - 1
        v = ex[p]
        v = jnp.where(lane24 == 64, pltpu.roll(zmid[0, xs], (-q) % 128, 1), v)
        v = jnp.where(lane24 == 127, pltpu.roll(zmid[1, xs], (127 - q) % 128, 1), v)
        ok = ok24 if x_ok is None else ok24 & x_ok
        mid_sums[p] = plane_sum(jnp.where(ok, v, 0.0))
    e1 = []
    for q in range(8):
        t = weigh(mid_sums, q + 1)[0:16]
        e = e_own[q][0:16]
        e1.append(0.2 * e + c1r[q + 1, 0:16] * (f1[q] + t - 2.0 * e))
    e1 = dot(jnp.concatenate(e1, axis=0), copy_mid).reshape(8, 16, 128)
    e1f[:, pl.ds(0, 16, 2), :] = e1
    e1f[:, pl.ds(1, 16, 2), :] = e1

    pltpu.make_async_copy(bf, bf, gsem.at[3]).wait()
    total = {}
    for j in range(gy):
        v = []
        for k in range(3):
            even = jnp.where(row8 < 7, pltpu.roll(bf[k, 0, j], 7, 0), 0.0)
            odd = jnp.where(row8 > 0, pltpu.roll(bf[k, 1, j], 1, 0), 0.0)
            v.append(even + odd)
        for yy in range(6):
            y = 4 * j + yy - 1
            if not 0 <= y < 32:
                continue
            w = None
            for k in range(3):
                at = (lane8 - (20 * yy + 16 * k) + 256) % 128
                part = jnp.where(at < 18, v[k], 0.0)
                w = part if w is None else w + part
            w = pltpu.roll(w, (64 * (y // 16) - 20 * yy - 1) % 128, 1)
            total[y] = total[y] + w if y in total else w
    for m in range(16):
        cof[m] = jnp.where(z_ok, jnp.where(low, total[m], total[m + 16]), 0.0)
        cov[m] = coc[m] * cof[m]

    def coarse(i, v):
        wrap_up = jnp.where(low, 0.0, pltpu.roll(v[15], 64, 1))
        wrap_down = jnp.where(low, pltpu.roll(v[0], 64, 1), 0.0)
        new = []
        for m in range(16):
            up = v[m - 1] if m else wrap_up
            down = v[m + 1] if m < 15 else wrap_down
            a = up + down + 2.0 * v[m]
            b = 2.0 * a + jnp.where(row8 == 0, 0.0, pltpu.roll(a, 1, 0)) + jnp.where(row8 == 7, 0.0, pltpu.roll(a, 7, 0))
            t = 2.0 * b + pltpu.roll(b, 1, 1) + pltpu.roll(b, 127, 1)
            new.append(0.2 * v[m] + coc[m] * (cof[m] + 0.25 * t - 2.0 * v[m]))
        return tuple(new)

    v = lax.fori_loop(0, ITERS - 1, coarse, tuple(cov[m] for m in range(16)))
    for m in range(16):
        cov[m] = v[m]

    mine = cov[pl.ds(4 * lax.rem(iy, 4), 4)]
    mine = mine.reshape(32, 128)
    mine = jnp.where(iy < 4, pltpu.roll(mine, 112, 1), pltpu.roll(mine, 48, 1))
    eout[...] = dot(mine, copy_coarse).reshape(4, 8, 128)
    for xc in range(2):
        for t in range(4):
            e3 = jnp.broadcast_to(eout[t, pl.ds(2 * ix + xc, 1), :], (8, 128))
            for p in range(8 * xc, 8 * xc + 8):
                rows = slice(8 * t, 8 * t + 8)
                out[p, rows, :] = vb[3 + p, rows, 0:NZ] + e1f[p // 2, rows, :] + e3

    for copy in fine_copies + mid_copies:
        copy.wait_send()
    pltpu.make_async_copy(dummy_c, dummy_c, gsem.at[0]).wait()
    pltpu.make_async_copy(dummy_f, dummy_f, gsem.at[2]).wait()


def on_device(sizes, guess, right_side, screen):
    vm = pltpu.VMEM
    n_peers = sizes[0] * sizes[1] * 3 - 1
    return pl.pallas_call(
        functools.partial(kernel, sizes),
        out_shape=jax.ShapeDtypeStruct((NX, NY, NZ), F32),
        in_specs=[pl.BlockSpec(memory_space=pltpu.HBM)] * 3,
        out_specs=pl.BlockSpec(memory_space=pltpu.VMEM),
        scratch_shapes=[
            vm((3, PX, PY, PZ), F32),
            vm((PX, PY, PZ), F32),
            vm((PX, PY, PZ), F32),
            vm((PX, PY, PZ), F32),
            vm((2, NY, 128), F32),
            vm((2, 3, PY, 128), F32),
            vm((8, NY, 128), F32),
            vm((2, 10, PY, 128), F32),
            vm((2, 10, 24, 128), F32),
            vm((10, 24, 128), F32),
            vm((10, 24, 128), F32),
            vm((10, 24, 128), F32),
            vm((16, 128), F32),
            vm((2, 3, 24, 128), F32),
            vm((8, NY, 128), F32),
            vm((3, 4, 128), F32),
            vm((3, 2, 128), F32),
            vm((3, 2, 8, 8, 128), F32),
            vm((3, 8, 8, 128), F32),
            vm((16, 8, 128), F32),
            vm((16, 8, 128), F32),
            vm((16, 8, 128), F32),
            vm((4, 8, 128), F32),
            vm((n_peers, 4, 128), F32),
            vm((n_peers, 2, 128), F32),
            pltpu.SemaphoreType.DMA((3,)),
            pltpu.SemaphoreType.DMA((30,)),
            pltpu.SemaphoreType.DMA((30,)),
            pltpu.SemaphoreType.DMA((26,)),
            pltpu.SemaphoreType.DMA((26,)),
            pltpu.SemaphoreType.DMA((4,)),
        ],
        compiler_params=pltpu.CompilerParams(
            collective_id=0, has_side_effects=True, vmem_limit_bytes=48 * 1024 * 1024
        ),
        name="multigrid",
    )(guess, right_side, screen)


def solution(mesh):
    placed = P("gx", "gy", "gz")
    sizes = tuple(mesh.shape[a] for a in ("gx", "gy", "gz"))
    return jax.shard_map(
        functools.partial(on_device, sizes), mesh=mesh, in_specs=(placed,) * 3, out_specs=placed, check_vma=False
    )
```

time: 564 us -> 38 us (0.07)
  the two profiles are of different devices: /device:TPU:32 before, /device:TPU:1 now
where the time goes in v1:
time: 38 us; the launch traced here: 37.8 us
  Pallas kernels  34.3 us (90%)
  local copies, waits for them, and re-layouts  3.55 us (9%)
    pallas_call x1, Pallas kernels, on_device(): pl.pallas_call(functools.partial(kernel, sizes), out_shape=jax.ShapeDtype...  34.3 us
    unnamed x7, local copies, waits for them, and re-layouts  3.55 us

profile of v1, /device:TPU:1, one launch (start us, length us, event | category | flops | bytes accessed | tf_op | source)
XLA Modules:
  0.0 37.8 jit_solution(2262786626295791675)
XLA Ops:
  0.0 0.0 copy-start
  0.0 0.9 %copy-done = f32[16,32,128]{2,1,0:T(8,128)S(1)} copy-done((f32[16,32,128]{2,1,0:T(8,128)S(1)}, f32[16,32,128]{2,1,0:T(8,128)}, u32[]{:S(2)}) %copy-start) | copy-done | bytes 262168
  1.0 0.0 copy-start.1
  1.0 0.9 %copy-done.1 = f32[16,32,128]{2,1,0:T(8,128)S(1)} copy-done((f32[16,32,128]{2,1,0:T(8,128)S(1)}, f32[16,32,128]{2,1,0:T(8,128)}, u32[]{:S(2)}) %copy-start.1) | copy-done | bytes 262168
  1.9 0.0 copy-start.2
  1.9 0.9 %copy-done.2 = f32[16,32,128]{2,1,0:T(8,128)S(1)} copy-done((f32[16,32,128]{2,1,0:T(8,128)S(1)}, f32[16,32,128]{2,1,0:T(8,128)}, u32[]{:S(2)}) %copy-start.2) | copy-done | bytes 262168
  2.9 34.3 %multigrid.1 = f32[16,32,128]{2,1,0:T(8,128)S(1)} custom-call(f32[16,32,128]{2,1,0:T(8,128)S(1)} %copy-done, f32[16,32,128]{2,1,0:T(8,128)S(1)} %copy-done.1, f32[16,32,128]{2,1,0:T(8,128)S(1)} %copy-done.2), custom_call_target="tpu_custom_call" | custom-call | tf_op jit(solution)/shard_map/multigrid/pallas_call | solution.py:488
  37.1 0.7 %copy.5 = f32[16,32,128]{2,1,0:T(8,128)} copy(f32[16,32,128]{2,1,0:T(8,128)S(1)} %multigrid.1) | data formatting | bytes 524288
Async XLA Ops:
  0.0 0.9 %copy-start = (f32[16,32,128]{2,1,0:T(8,128)S(1)}, f32[16,32,128]{2,1,0:T(8,128)}, u32[]{:S(2)}) copy-start(f32[16,32,128]{2,1,0:T(8,128)} %guess.1) | copy-start | bytes 786436
  1.0 0.9 %copy-start.1 = (f32[16,32,128]{2,1,0:T(8,128)S(1)}, f32[16,32,128]{2,1,0:T(8,128)}, u32[]{:S(2)}) copy-start(f32[16,32,128]{2,1,0:T(8,128)} %rhs.1) | copy-start | bytes 786436
  1.9 0.9 %copy-start.2 = (f32[16,32,128]{2,1,0:T(8,128)S(1)}, f32[16,32,128]{2,1,0:T(8,128)}, u32[]{:S(2)}) copy-start(f32[16,32,128]{2,1,0:T(8,128)} %scr.1) | copy-start | bytes 786436

commit v2 on v1

--- a/solution.py
+++ b/solution.py
@@ -13,7 +13,6 @@
 CENTER = 14.0
 F32 = jnp.float32
 MESH = pl.DeviceIdType.MESH
-HIGH = lax.Precision.HIGHEST
 
 NX, NY, NZ = 16, 32, 128
 PX, PY, PZ = 22, 40, 256
@@ -58,16 +57,14 @@
     zpack,
     zmid,
     e1f,
+    base,
     msg,
-    cmsg,
     bf,
-    bc,
     cof,
     coc,
     cov,
     eout,
-    dummy_f,
-    dummy_c,
+    dummy,
     load_sem,
     fs,
     fr,
@@ -91,26 +88,58 @@
         if o != (0, 0, 0)
     ]
     peers = [(a - gx if a > gx // 2 else a, b - gy if b > gy // 2 else b, c) for a, b, c in peers]
-    peers.sort(key=lambda o: -(abs(o[0]) + (abs(o[1]) + 1) // 2 + abs(o[2])))
+
+    def hops(o):
+        return abs(o[0]) + (abs(o[1]) + 1) // 2 + abs(o[2])
+
+    peers.sort(key=lambda o: -hops(o))
+
+    def has(dz):
+        return iz < gz - 1 if dz == 1 else iz > 0
+
+    def by_side(offsets, act):
+        for o in offsets:
+            if o[2] == 0:
+                act(o)
+        for dz in (1, -1):
+
+            @pl.when(has(dz))
+            def _(dz=dz):
+                for o in offsets:
+                    if o[2] == dz:
+                        act(o)
+
+    heard = [(1, 3, 0), (1, 2, 0), (1, -2, 0), (0, 3, 0), (0, 2, 0), (0, -2, 0)] + NEIGHBOURS
+    barrier = pltpu.get_barrier_semaphore()
+    by_side(
+        [(-o[0], -o[1], -o[2]) for o in heard],
+        lambda o: pl.semaphore_signal(barrier, inc=1, device_id=device(o), device_id_type=MESH),
+    )
+    sides = (iz > 0).astype(jnp.int32) + (iz < gz - 1).astype(jnp.int32)
 
     own = []
-    for a, ref in enumerate((scr, rhs, guess)):
-        copy = pltpu.make_async_copy(ref, mm.at[2 - a, pl.ds(3, NX), pl.ds(0, NY), pl.ds(0, NZ)], load_sem.at[a])
+    for a, ref in ((2, scr), (0, guess), (1, rhs)):
+        copy = pltpu.make_async_copy(ref, mm.at[a, pl.ds(3, NX), pl.ds(0, NY), pl.ds(0, NZ)], load_sem.at[a])
         copy.start()
         own.append(copy)
     for a in range(3):
         for p in range(PX):
-            mm[a, p, NY:PY, 0:NZ] = jnp.zeros((PY - NY, NZ), F32)
+            mm[a, p, NY + 3 : PY - 3, 0:NZ] = jnp.zeros((PY - NY - 6, NZ), F32)
     for side in range(2):
         for xs in range(3):
-            zland[side, xs, NY:PY, :] = jnp.zeros((PY - NY, 128), F32)
-            zmid[side, xs, 16:24, :] = jnp.zeros((8, 128), F32)
-    ex[...] = jnp.zeros_like(ex)
+            zland[side, xs, NY + 3 : PY - 3, :] = jnp.zeros((PY - NY - 6, 128), F32)
+            zmid[side, xs, 17:23, :] = jnp.zeros((6, 128), F32)
+    for q in range(10):
+        ex[q, 17:23, :] = jnp.zeros((6, 128), F32)
     s24[...] = jnp.zeros_like(s24)
 
-    barrier = pltpu.get_barrier_semaphore()
-    for o in peers:
-        pl.semaphore_signal(barrier, inc=1, device_id=device(o), device_id_type=MESH)
+    for side, dz in ((0, 1), (1, -1)):
+
+        @pl.when(jnp.logical_not(has(dz)))
+        def _(side=side, dz=dz):
+            zland[side] = jnp.zeros((3, PY, 128), F32)
+            zmid[side] = jnp.zeros((3, 24, 128), F32)
+            bf[1 + dz] = jnp.zeros((gy, gx, 8, 128), F32)
 
     r_i, c_i = iota((128, 128), 0), iota((128, 128), 1)
     pool = jnp.where(r_i // 2 == c_i, 0.5, 0.0).astype(F32)
@@ -124,23 +153,17 @@
     gather_c = jnp.where((r_i // 4 == c_i % 16) & (r_i < 64), 0.25, 0.0).astype(F32)
 
     def dot(a, b):
-        return jnp.dot(a, b, precision=HIGH, preferred_element_type=F32)
+        b = b.astype(jnp.bfloat16)
+        total = None
+        for i in range(3):
+            part = a.astype(jnp.bfloat16)
+            term = jnp.dot(part, b, preferred_element_type=F32)
+            total = term if total is None else total + term
+            a = a - part.astype(F32)
+        return total
 
     for copy in own:
         copy.wait()
-
-    for q in range(8):
-        rx[q] = mm[2, 3 + 2 * q, 0:NY, 0:NZ] + mm[2, 4 + 2 * q, 0:NY, 0:NZ]
-    s1_own = dot((rx[:, pl.ds(0, 16, 2), :] + rx[:, pl.ds(1, 16, 2), :]).reshape(128, 128), pool).reshape(8, 16, 128)
-    lanes16 = iota((16, 128), 1)
-    rows16 = iota((16, 128), 0)
-    for xc in range(2):
-        s4 = s1_own[4 * xc] + s1_own[4 * xc + 1] + s1_own[4 * xc + 2] + s1_own[4 * xc + 3]
-        s4 = dot(s4, gather_c)
-        s3 = jnp.sum(jnp.where((lanes16 // 16) % 4 == rows16 // 4, s4, 0.0), axis=0, keepdims=True)
-        c3 = OMEGA / (CENTER + s3)
-        for k in range(3):
-            cmsg[k, xc : xc + 1, :] = c3 if k == 0 else pltpu.roll(c3, 16 * k, 1)
 
     lane = iota((NY, 128), 1)
     head = jnp.zeros((NY, 128), F32)
@@ -163,17 +186,40 @@
     packs[0] = head
     packs[1] = tail
 
-    pl.semaphore_wait(barrier, len(peers))
+    pl.semaphore_wait(barrier, len(heard) - 18 + 9 * sides)
 
     fine_copies = []
-
-    def send_fine(o, src, dst):
-        i = len(fine_copies)
-        copy = pltpu.make_async_remote_copy(
-            src_ref=src, dst_ref=dst, send_sem=fs.at[i], recv_sem=fr.at[i], device_id=device(o), device_id_type=MESH
+    given = (guess, rhs, scr)
+
+    def describe(o, refs, sems, i):
+        src, dst = refs()
+        return pltpu.make_async_remote_copy(
+            src_ref=src,
+            dst_ref=dst,
+            send_sem=sems[0].at[i],
+            recv_sem=sems[1].at[i],
+            device_id=device(o),
+            device_id_type=MESH,
         )
-        copy.start()
-        fine_copies.append(copy)
+
+    def send_fine(o, refs):
+        fine_copies.append((o, refs, (fs, fr), len(fine_copies)))
+        describe(*fine_copies[-1]).start()
+
+    def finish(copies, sending):
+        def one(copy):
+            describe(*copy).wait_send() if sending else describe(*copy).wait_recv()
+
+        for copy in copies:
+            if copy[0][2] == 0:
+                one(copy)
+        for dz in (1, -1):
+
+            @pl.when(has(dz if sending else -dz))
+            def _(dz=dz):
+                for copy in copies:
+                    if copy[0][2] == dz:
+                        one(copy)
 
     def x_part(d, depth):
         if d == 0:
@@ -190,48 +236,69 @@
             (p0, n), (q0, _) = x_part(o[0], depth)
             send_fine(
                 o,
-                mm.at[a, pl.ds(p0, n), pl.ds(0, NY), pl.ds(0, NZ)],
-                mm.at[a, pl.ds(q0, n), pl.ds(0, NY), pl.ds(0, NZ)],
+                lambda a=a, p0=p0, n=n, q0=q0: (
+                    given[a].at[pl.ds(p0 - 3, n)],
+                    mm.at[a, pl.ds(q0, n), pl.ds(0, NY), pl.ds(0, NZ)],
+                ),
             )
     for o in NEIGHBOURS:
         dx, dy, dz = o
+        if dz == 0 and dx != 0 and dy != 0:
+            (s0, sn), (t0, _) = y_part(dy, 3)
+            (p0, n), (q0, _) = x_part(dx, 3)
+            for a in range(3):
+                send_fine(
+                    o,
+                    lambda a=a, p0=p0, n=n, q0=q0, s0=s0, sn=sn, t0=t0: (
+                        given[a].at[pl.ds(p0 - 3, n), pl.ds(s0, sn), :],
+                        mm.at[a, pl.ds(q0, n), pl.ds(t0, sn), pl.ds(0, NZ)],
+                    ),
+                )
+
+    for o in NEIGHBOURS:
+        dx, dy, dz = o
+        if dz == 0 and dx == 0:
+            (s0, sn), (t0, _) = y_part(dy, 3)
+            (p0, n), (q0, _) = x_part(dx, 3)
+            for a in range(3):
+                send_fine(
+                    o,
+                    lambda a=a, p0=p0, n=n, q0=q0, s0=s0, sn=sn, t0=t0: (
+                        given[a].at[pl.ds(p0 - 3, n), pl.ds(s0, sn), :],
+                        mm.at[a, pl.ds(q0, n), pl.ds(t0, sn), pl.ds(0, NZ)],
+                    ),
+                )
+
+    def send_pack(o):
+        dx, dy, dz = o
         (s0, sn), (t0, _) = y_part(dy, 3)
-        if dz == 0:
-            if dy == 0:
-                continue
-            (p0, n), (q0, _) = x_part(dx, 3)
-            send_fine(
-                o,
-                mm.at[:, pl.ds(p0, n), pl.ds(s0, sn), pl.ds(0, NZ)],
-                mm.at[:, pl.ds(q0, n), pl.ds(t0, sn), pl.ds(0, NZ)],
-            )
-        else:
-            side = 1 if dz == 1 else 0
-            send_fine(o, packs.at[side, pl.ds(s0, sn), :], zland.at[side, 1 - dx, pl.ds(t0, sn), :])
-
-    c_copies = []
-    for o in peers:
-        copy = pltpu.make_async_remote_copy(
-            src_ref=cmsg.at[1 - o[2]],
-            dst_ref=bc.at[1 - o[2], iy, pl.ds(2 * ix, 2), :],
-            send_sem=gsem.at[0],
-            recv_sem=gsem.at[1],
-            device_id=device(o),
-            device_id_type=MESH,
+        side = 1 if dz == 1 else 0
+        send_fine(
+            o, lambda: (packs.at[side, pl.ds(s0, sn), :], zland.at[side, 1 - dx, pl.ds(t0, sn), :])
         )
-        copy.start()
-        c_copies.append(copy)
-    pltpu.make_async_copy(cmsg.at[1], bc.at[1, iy, pl.ds(2 * ix, 2), :], gsem.at[1]).start()
-
-    for copy in fine_copies:
-        copy.wait_recv()
+
+    by_side([o for o in sorted(NEIGHBOURS, key=lambda o: o[0] != 0) if o[2] != 0], send_pack)
+
+    for q in range(8):
+        rx[q] = mm[2, 3 + 2 * q, 0:NY, 0:NZ] + mm[2, 4 + 2 * q, 0:NY, 0:NZ]
+    s1_own = dot((rx[:, pl.ds(0, 16, 2), :] + rx[:, pl.ds(1, 16, 2), :]).reshape(128, 128), pool).reshape(8, 16, 128)
+    lanes16 = iota((16, 128), 1)
+    rows16 = iota((16, 128), 0)
+    s4 = [s1_own[4 * i] + s1_own[4 * i + 1] + s1_own[4 * i + 2] + s1_own[4 * i + 3] for i in range(2)]
+    s4 = dot(jnp.concatenate(s4, axis=0), gather_c)
+    s4 = [jnp.where(lanes16 // 16 == rows16 // 4 + 4 * i, s4[16 * i : 16 * i + 16], 0.0) for i in range(2)]
+    c3 = OMEGA / (CENTER + jnp.sum(s4[0] + s4[1], axis=0, keepdims=True))
+    for k in range(3):
+        msg[k, 4:5, :] = c3 if k == 0 else pltpu.roll(c3, 16 * k, 1)
+
+    finish([c for c in fine_copies if c[0][0] == 0], False)
 
     rows_in = iota((PY, 128), 0)
     lane40 = iota((PY, 128), 1)
     row_ok = ((rows_in < 36) | (iy > 0)) & ((rows_in < NY) | (rows_in >= 36) | (iy < gy - 1))
     col_ok = ((lane40 < 64) & (iz < gz - 1)) | ((lane40 >= 64) & (iz > 0))
     both_ok = row_ok & col_ok
-    for p in range(PX):
+    def columns(p):
         if p < 3:
             xs, q, x_ok = 0, NX - 3 + p, ix > 0
         elif p < 3 + NX:
@@ -259,45 +326,57 @@
             cc[p, :, 0:NZ] = jnp.where(ok0, OMEGA / (CENTER + mm[2, p, :, 0:NZ]), 0.0)
             cc[p, :, NZ:PZ] = jnp.where(ok1, OMEGA / (CENTER + s1), 0.0)
 
-    def sweep(src, dst, first, last):
+    for p in range(3, 3 + NX):
+        columns(p)
+
+    def update(src, dst, p, b0, b1, b2):
+        v = src[p]
+        t = b0 + b1 + b1 + b2
+        dst[p] = 0.2 * v + cc[p] * (mm[1, p] + 0.25 * t - 2.0 * v)
+
+    def inner(src, dst, first, last):
         def body(p, carry):
             b0, b1 = carry
             b2 = plane_sum(src[p + 1])
-            v = src[p]
-            t = b0 + b1 + b1 + b2
-            dst[p] = 0.2 * v + cc[p] * (mm[1, p] + 0.25 * t - 2.0 * v)
+            update(src, dst, p, b0, b1, b2)
             return b1, b2
 
-        lax.fori_loop(first, last, body, (plane_sum(src[first - 1]), plane_sum(src[first])), unroll=2)
-
-    sweep(mm.at[0], va, 1, PX - 1)
-    sweep(va, vb, 2, PX - 2)
-
-    def residual(p, b0, b1):
-        b2 = plane_sum(vb[p + 1])[0:NY, 0:NZ]
+        b0, b1 = plane_sum(src[first - 1]), plane_sum(src[first])
+        b2, b3 = b0, b1
+        for p in range(first, last):
+            b2, b3 = body(p, (b2, b3))
+        return {first - 1: b0, first: b1, last - 1: b2, last: b3}
+
+    def outer(src, dst, planes, sums):
+        for p in planes:
+            for i in (p - 1, p, p + 1):
+                if i not in sums:
+                    sums[i] = plane_sum(src[i])
+            update(src, dst, p, sums[p - 1], sums[p], sums[p + 1])
+
+    def own_sum(p):
+        return plane_sum(vb[p])[0:NY, 0:NZ]
+
+    def residual(p, b0, b1, b2):
         t = b0 + b1 + b1 + b2
         v = vb[p, 0:NY, 0:NZ]
-        return mm[1, p, 0:NY, 0:NZ] - (CENTER + 2.0 + mm[2, p, 0:NY, 0:NZ]) * v + 0.25 * t, b2
+        return mm[1, p, 0:NY, 0:NZ] - (CENTER + 2.0 + mm[2, p, 0:NY, 0:NZ]) * v + 0.25 * t
 
     def pair(q, carry):
         b0, b1 = carry
-        r0, b2 = residual(3 + 2 * q, b0, b1)
-        r1, b3 = residual(4 + 2 * q, b1, b2)
-        rx[q] = r0 + r1
+        b2 = own_sum(4 + 2 * q)
+        b3 = own_sum(5 + 2 * q)
+        rx[q] = residual(3 + 2 * q, b0, b1, b2) + residual(4 + 2 * q, b1, b2, b3)
         return b2, b3
 
-    lax.fori_loop(0, 8, pair, (plane_sum(vb[2])[0:NY, 0:NZ], plane_sum(vb[3])[0:NY, 0:NZ]))
-    f1 = dot((rx[:, pl.ds(0, 16, 2), :] + rx[:, pl.ds(1, 16, 2), :]).reshape(128, 128), pool).reshape(8, 16, 128)
-
-    for q in range(10):
-        sx[0, q] = mm[2, 1 + 2 * q, :, 0:NZ] + mm[2, 2 + 2 * q, :, 0:NZ]
-        sx[1, q] = mm[2, 1 + 2 * q, :, NZ:PZ] + mm[2, 2 + 2 * q, :, NZ:PZ]
-    for half in range(2):
-        v = sx[half, :, pl.ds(0, 20, 2), :] + sx[half, :, pl.ds(1, 20, 2), :]
-        s24[half, :, 0:20, :] = v
-        s24[half, :, 23:24, :] = v[:, 19:20, :]
-    s1 = dot(s24[0].reshape(240, 128), pool) + dot(s24[1].reshape(240, 128), pool_halo)
-    s1 = s1.reshape(10, 24, 128)
+    first_sums = inner(mm.at[0], va, 4, 18)
+    second_sums = inner(va, vb, 5, 17)
+    third_sums = {6: own_sum(6), 7: own_sum(7)}
+    sums = third_sums[6], third_sums[7]
+    for q in range(2, 6):
+        sums = pair(q, sums)
+    third_sums[14], third_sums[15] = sums
+
     row24, lane24 = iota((24, 128), 0), iota((24, 128), 1)
     ok24 = (
         ((row24 < 20) | (iy > 0))
@@ -305,10 +384,40 @@
         & ((lane24 < 96) | (iz > 0))
         & ((lane24 < 64) | (lane24 >= 96) | (iz < gz - 1))
     )
-    for q in range(10):
-        ok = ok24 & (ix > 0) if q == 0 else (ok24 & (ix < gx - 1) if q == 9 else ok24)
-        s1r[q] = s1[q]
-        c1r[q] = jnp.where(ok, OMEGA / (CENTER + s1[q]), 0.0)
+
+    def mid_screen(planes):
+        for q in planes:
+            sx[0, q] = mm[2, 1 + 2 * q, :, 0:NZ] + mm[2, 2 + 2 * q, :, 0:NZ]
+            sx[1, q] = mm[2, 1 + 2 * q, :, NZ:PZ] + mm[2, 2 + 2 * q, :, NZ:PZ]
+            for half in range(2):
+                v = sx[half, q, pl.ds(0, 20, 2), :] + sx[half, q, pl.ds(1, 20, 2), :]
+                s24[half, q, 0:20, :] = v
+                s24[half, q, 23:24, :] = v[19:20, :]
+        a = [jnp.concatenate([s24[half, q] for q in planes], axis=0) for half in range(2)]
+        s1 = dot(a[0], pool) + dot(a[1], pool_halo)
+        for i, q in enumerate(planes):
+            ok = ok24 & (ix > 0) if q == 0 else (ok24 & (ix < gx - 1) if q == 9 else ok24)
+            s1r[q] = s1[24 * i : 24 * i + 24]
+            c1r[q] = jnp.where(ok, OMEGA / (CENTER + s1[24 * i : 24 * i + 24]), 0.0)
+
+    mid_screen(tuple(range(1, 9)))
+
+    finish([c for c in fine_copies if c[0][0] != 0], False)
+
+    for p in (0, 1, 2, 19, 20, 21):
+        columns(p)
+    outer(mm.at[0], va, (3, 2, 1, 18, 19, 20), first_sums)
+    outer(va, vb, (4, 3, 2, 17, 18, 19), second_sums)
+    for q in (1, 0, 6, 7):
+        for i in range(2 + 2 * q, 6 + 2 * q):
+            if i not in third_sums:
+                third_sums[i] = own_sum(i)
+        b = [third_sums[i] for i in range(2 + 2 * q, 6 + 2 * q)]
+        rx[q] = residual(3 + 2 * q, *b[:3]) + residual(4 + 2 * q, *b[1:])
+
+    mid_screen((0, 9))
+
+    f1 = dot((rx[:, pl.ds(0, 16, 2), :] + rx[:, pl.ds(1, 16, 2), :]).reshape(128, 128), pool).reshape(8, 16, 128)
 
     zero8 = jnp.zeros((8, 128), F32)
     f1z = [jnp.concatenate([f1[q], zero8], axis=0) for q in range(8)]
@@ -347,18 +456,22 @@
         for k in range(3):
             msg[k, i : i + 1, :] = row if k == 0 else pltpu.roll(row, 16 * k, 1)
 
-    slot = bf.at[:, lax.rem(ix, 2), iy, pl.ds(4 * (ix // 2), 4), :]
-    for o in peers:
-        copy = pltpu.make_async_remote_copy(
-            src_ref=msg.at[1 - o[2]],
-            dst_ref=slot.at[1 - o[2]],
-            send_sem=gsem.at[2],
-            recv_sem=gsem.at[3],
-            device_id=device(o),
-            device_id_type=MESH,
-        )
-        copy.start()
-    pltpu.make_async_copy(msg.at[1], slot.at[1], gsem.at[3]).start()
+    slot = bf.at[:, iy, ix, pl.ds(0, 5), :]
+    def send_parts(to):
+        def one(o):
+            pltpu.make_async_remote_copy(
+                src_ref=msg.at[1 - o[2]],
+                dst_ref=slot.at[1 - o[2]],
+                send_sem=gsem.at[1 + o[2]],
+                recv_sem=gsem.at[4 - o[2]],
+                device_id=device(o),
+                device_id_type=MESH,
+            ).start()
+
+        by_side(to, one)
+
+    send_parts([o for o in peers if hops(o) > 2])
+    pltpu.make_async_copy(msg.at[1], slot.at[1], gsem.at[4]).start()
 
     ztail = jnp.zeros((16, 128), F32)
     for q in range(8):
@@ -366,43 +479,30 @@
         ztail = jnp.where(lanes16 == 64 + q, pltpu.roll(e_own[q][0:16], 64 + q, 1), ztail)
     zpack[...] = ztail
     mid_copies = []
-    for o in NEIGHBOURS:
+
+    def send_mid(o):
         dx, dy, dz = o
         (s0, sn), t0 = ((0, 16), 0) if dy == 0 else (((15, 1), 23) if dy == 1 else ((0, 1), 16))
         if dz == 0:
             (p0, n), q0 = ((1, 8), 1) if dx == 0 else (((8, 1), 0) if dx == 1 else ((1, 1), 9))
-            src = ex.at[pl.ds(p0, n), pl.ds(s0, sn), :]
-            dst = ex.at[pl.ds(q0, n), pl.ds(t0, sn), :]
+
+            def refs():
+                return ex.at[pl.ds(p0, n), pl.ds(s0, sn), :], ex.at[pl.ds(q0, n), pl.ds(t0, sn), :]
+
         else:
             side = 1 if dz == 1 else 0
-            src = zpack.at[pl.ds(s0, sn), :]
-            dst = zmid.at[side, 1 - dx, pl.ds(t0, sn), :]
-        i = len(mid_copies)
-        copy = pltpu.make_async_remote_copy(
-            src_ref=src, dst_ref=dst, send_sem=ms.at[i], recv_sem=mr.at[i], device_id=device(o), device_id_type=MESH
-        )
-        copy.start()
-        mid_copies.append(copy)
-
-    pltpu.make_async_copy(bc, bc, gsem.at[1]).wait()
-    lane8, row8 = iota((8, 128), 1), iota((8, 128), 0)
-    block = (lane8 // 16) % 4
-    z_ok = (block < 3) & ((block > 0) | (iz > 0)) & ((block < 2) | (iz < gz - 1))
-    low = lane8 < 64
-    half = {}
-    for y in range(32):
-        j, yy = y // 4, y % 4
-        d = (lane8 // 16 - yy + 8) % 4
-        v = jnp.where(d == 0, bc[0, j], jnp.where(d == 1, bc[1, j], bc[2, j]))
-        if yy:
-            v = pltpu.roll(v, 128 - 16 * yy, 1)
-        if y < 16:
-            half[y] = v
-        else:
-            coc[y - 16] = jnp.where(z_ok, jnp.where(low, half[y - 16], v), 0.0)
-
-    for copy in mid_copies:
-        copy.wait_recv()
+
+            def refs():
+                return zpack.at[pl.ds(s0, sn), :], zmid.at[side, 1 - dx, pl.ds(t0, sn), :]
+
+        mid_copies.append((o, refs, (ms, mr), len(mid_copies)))
+        describe(*mid_copies[-1]).start()
+
+    by_side(NEIGHBOURS, send_mid)
+
+    send_parts([o for o in peers if hops(o) <= 2])
+
+    finish(mid_copies, False)
     mid_sums = {}
     for p in range(10):
         if p == 0:
@@ -424,15 +524,41 @@
     e1 = dot(jnp.concatenate(e1, axis=0), copy_mid).reshape(8, 16, 128)
     e1f[:, pl.ds(0, 16, 2), :] = e1
     e1f[:, pl.ds(1, 16, 2), :] = e1
-
-    pltpu.make_async_copy(bf, bf, gsem.at[3]).wait()
-    total = {}
+    for p in range(NX):
+        base[p] = vb[3 + p, 0:NY, 0:NZ] + e1f[p // 2]
+
+    def wait_parts(k):
+        landed = bf.at[k, :, :, pl.ds(0, 5), :]
+        pltpu.make_async_copy(landed, landed, gsem.at[3 + k]).wait()
+
+    wait_parts(1)
+    for k in (0, 2):
+        pl.when(has(k - 1))(functools.partial(wait_parts, k))
+
+    lane8, row8 = iota((8, 128), 1), iota((8, 128), 0)
+    block = (lane8 // 16) % 4
+    z_ok = (block < 3) & ((block > 0) | (iz > 0)) & ((block < 2) | (iz < gz - 1))
+    low = lane8 < 64
+    total, screens = {}, {}
     for j in range(gy):
-        v = []
+        v, c = [], []
         for k in range(3):
-            even = jnp.where(row8 < 7, pltpu.roll(bf[k, 0, j], 7, 0), 0.0)
-            odd = jnp.where(row8 > 0, pltpu.roll(bf[k, 1, j], 1, 0), 0.0)
-            v.append(even + odd)
+            f = w = None
+            for i in range(gx):
+                tile = bf[k, j, i]
+                at = row8 - (2 * i - 1)
+                part = jnp.where((at >= 0) & (at < 4), pltpu.roll(tile, (2 * i - 1) % 8, 0), 0.0)
+                f = part if f is None else f + part
+                row = jnp.broadcast_to(tile[4:5], (8, 128))
+                w = row if w is None else jnp.where(row8 < 2 * i, w, row)
+            v.append(f)
+            c.append(jnp.where(row8 % 2 == 0, w, pltpu.roll(w, 64, 1)))
+        for yy in range(4):
+            d = (lane8 // 16 - yy + 8) % 8
+            w = jnp.where(d == 0, c[0], jnp.where(d == 1, c[1], c[2]))
+            y = 4 * j + yy
+            shift = (64 * (y // 16) - 16 * yy) % 128
+            screens[y] = pltpu.roll(w, shift, 1) if shift else w
         for yy in range(6):
             y = 4 * j + yy - 1
             if not 0 <= y < 32:
@@ -446,6 +572,7 @@
             total[y] = total[y] + w if y in total else w
     for m in range(16):
         cof[m] = jnp.where(z_ok, jnp.where(low, total[m], total[m + 16]), 0.0)
+        coc[m] = jnp.where(z_ok, jnp.where(low, screens[m], screens[m + 16]), 0.0)
         cov[m] = coc[m] * cof[m]
 
     def coarse(i, v):
@@ -474,17 +601,21 @@
             e3 = jnp.broadcast_to(eout[t, pl.ds(2 * ix + xc, 1), :], (8, 128))
             for p in range(8 * xc, 8 * xc + 8):
                 rows = slice(8 * t, 8 * t + 8)
-                out[p, rows, :] = vb[3 + p, rows, 0:NZ] + e1f[p // 2, rows, :] + e3
-
-    for copy in fine_copies + mid_copies:
-        copy.wait_send()
-    pltpu.make_async_copy(dummy_c, dummy_c, gsem.at[0]).wait()
-    pltpu.make_async_copy(dummy_f, dummy_f, gsem.at[2]).wait()
+                out[p, rows, :] = base[p, rows, :] + e3
+
+    finish(fine_copies + mid_copies, True)
+
+    def wait_sent(dz):
+        sent = dummy.at[pl.ds(0, gx * gy - (dz == 0)), pl.ds(0, 5), :]
+        pltpu.make_async_copy(sent, sent, gsem.at[1 + dz]).wait()
+
+    wait_sent(0)
+    for dz in (1, -1):
+        pl.when(has(dz))(functools.partial(wait_sent, dz))
 
 
 def on_device(sizes, guess, right_side, screen):
     vm = pltpu.VMEM
-    n_peers = sizes[0] * sizes[1] * 3 - 1
     return pl.pallas_call(
         functools.partial(kernel, sizes),
         out_shape=jax.ShapeDtypeStruct((NX, NY, NZ), F32),
@@ -506,25 +637,23 @@
             vm((16, 128), F32),
             vm((2, 3, 24, 128), F32),
             vm((8, NY, 128), F32),
-            vm((3, 4, 128), F32),
-            vm((3, 2, 128), F32),
-            vm((3, 2, 8, 8, 128), F32),
-            vm((3, 8, 8, 128), F32),
+            vm((NX, NY, NZ), F32),
+            vm((3, 5, 128), F32),
+            vm((3, sizes[1], sizes[0], 8, 128), F32),
             vm((16, 8, 128), F32),
             vm((16, 8, 128), F32),
             vm((16, 8, 128), F32),
             vm((4, 8, 128), F32),
-            vm((n_peers, 4, 128), F32),
-            vm((n_peers, 2, 128), F32),
+            vm((sizes[0] * sizes[1], 8, 128), F32),
             pltpu.SemaphoreType.DMA((3,)),
-            pltpu.SemaphoreType.DMA((30,)),
-            pltpu.SemaphoreType.DMA((30,)),
+            pltpu.SemaphoreType.DMA((42,)),
+            pltpu.SemaphoreType.DMA((42,)),
             pltpu.SemaphoreType.DMA((26,)),
             pltpu.SemaphoreType.DMA((26,)),
-            pltpu.SemaphoreType.DMA((4,)),
+            pltpu.SemaphoreType.DMA((6,)),
         ],
         compiler_params=pltpu.CompilerParams(
-            collective_id=0, has_side_effects=True, vmem_limit_bytes=48 * 1024 * 1024
+            collective_id=0, has_side_effects=True, vmem_limit_bytes=60 * 1024 * 1024
         ),
         name="multigrid",
     )(guess, right_side, screen)

time: 38 us -> 28.3 us (0.74)
  the two profiles are of different devices: /device:TPU:1 before, /device:TPU:32 now
where the time goes in v2:
time: 28.3 us; the launch traced here: 27.9 us
  Pallas kernels  26.2 us (93%)
  local copies, waits for them, and re-layouts  1.67 us (6%)
    pallas_call x1, Pallas kernels, on_device(): pl.pallas_call(functools.partial(kernel, sizes), out_shape=jax.ShapeDtype...  26.2 us
    unnamed x1, local copies, waits for them, and re-layouts  1.67 us

profile of v2, /device:TPU:32, one launch (start us, length us, event | category | flops | bytes accessed | tf_op | source)
XLA Modules:
  0.0 27.9 jit_solution(9903154192208134526)
XLA Ops:
  0.0 26.2 %multigrid.1 = f32[16,32,128]{2,1,0:T(8,128)} custom-call(f32[16,32,128]{2,1,0:T(8,128)} %guess.1, f32[16,32,128]{2,1,0:T(8,128)} %rhs.1, f32[16,32,128]{2,1,0:T(8,128)} %scr.1), custom_call_target="tpu_custom_call" | custom-call | tf_op jit(solution)/shard_map/multigrid/pallas_call | solution.py:619
  26.2 1.7 %copy.5 = f32[16,32,128]{2,1,0:T(8,128)} copy(f32[16,32,128]{2,1,0:T(8,128)} %multigrid.1) | data formatting | bytes 524288

commit v3 on v2

--- a/solution.py
+++ b/solution.py
@@ -47,7 +47,9 @@
     va,
     vb,
     packs,
+    edges,
     zland,
+    eland,
     rx,
     sx,
     s24,
@@ -124,7 +126,8 @@
         own.append(copy)
     for a in range(3):
         for p in range(PX):
-            mm[a, p, NY + 3 : PY - 3, 0:NZ] = jnp.zeros((PY - NY - 6, NZ), F32)
+            depth = 2 if a else 3
+            mm[a, p, NY + depth : PY - depth, 0:NZ] = jnp.zeros((PY - NY - 2 * depth, NZ), F32)
     for side in range(2):
         for xs in range(3):
             zland[side, xs, NY + 3 : PY - 3, :] = jnp.zeros((PY - NY - 6, 128), F32)
@@ -138,6 +141,7 @@
         @pl.when(jnp.logical_not(has(dz)))
         def _(side=side, dz=dz):
             zland[side] = jnp.zeros((3, PY, 128), F32)
+            eland[side] = jnp.zeros((2, 8, 128), F32)
             zmid[side] = jnp.zeros((3, 24, 128), F32)
             bf[1 + dz] = jnp.zeros((gy, gx, 8, 128), F32)
 
@@ -162,30 +166,6 @@
             a = a - part.astype(F32)
         return total
 
-    for copy in own:
-        copy.wait()
-
-    lane = iota((NY, 128), 1)
-    head = jnp.zeros((NY, 128), F32)
-    tail = jnp.zeros((NY, 128), F32)
-    for p in range(NX):
-        g = mm[0, 3 + p, 0:NY, 0:NZ]
-        f = mm[1, 3 + p, 0:NY, 0:NZ]
-        s = mm[2, 3 + p, 0:NY, 0:NZ]
-
-        def put(acc, v, to, at, count):
-            first = 8 * p + to
-            return jnp.where((lane >= first) & (lane < first + count), pltpu.roll(v, (first - at) % 128, 1), acc)
-
-        head = put(head, g, 0, 0, 3)
-        head = put(head, f, 3, 0, 2)
-        head = put(head, s, 5, 0, 2)
-        tail = put(tail, g, 5, 125, 3)
-        tail = put(tail, f, 3, 126, 2)
-        tail = put(tail, s, 1, 126, 2)
-    packs[0] = head
-    packs[1] = tail
-
     pl.semaphore_wait(barrier, len(heard) - 18 + 9 * sides)
 
     fine_copies = []
@@ -231,51 +211,54 @@
             return (0, NY), (0, NY)
         return ((NY - depth, depth), (PY - depth, depth)) if d == 1 else ((0, depth), (NY, depth))
 
-    for o in ((1, 0, 0), (-1, 0, 0)):
+    def send_rows(o):
         for a, depth in ((0, 3), (1, 2), (2, 2)):
             (p0, n), (q0, _) = x_part(o[0], depth)
+            (s0, sn), (t0, _) = y_part(o[1], depth)
             send_fine(
                 o,
-                lambda a=a, p0=p0, n=n, q0=q0: (
-                    given[a].at[pl.ds(p0 - 3, n)],
-                    mm.at[a, pl.ds(q0, n), pl.ds(0, NY), pl.ds(0, NZ)],
+                lambda a=a, p0=p0, n=n, q0=q0, s0=s0, sn=sn, t0=t0: (
+                    given[a].at[pl.ds(p0 - 3, n), pl.ds(s0, sn), :],
+                    mm.at[a, pl.ds(q0, n), pl.ds(t0, sn), pl.ds(0, NZ)],
                 ),
             )
-    for o in NEIGHBOURS:
-        dx, dy, dz = o
-        if dz == 0 and dx != 0 and dy != 0:
-            (s0, sn), (t0, _) = y_part(dy, 3)
-            (p0, n), (q0, _) = x_part(dx, 3)
-            for a in range(3):
-                send_fine(
-                    o,
-                    lambda a=a, p0=p0, n=n, q0=q0, s0=s0, sn=sn, t0=t0: (
-                        given[a].at[pl.ds(p0 - 3, n), pl.ds(s0, sn), :],
-                        mm.at[a, pl.ds(q0, n), pl.ds(t0, sn), pl.ds(0, NZ)],
-                    ),
-                )
-
-    for o in NEIGHBOURS:
-        dx, dy, dz = o
-        if dz == 0 and dx == 0:
-            (s0, sn), (t0, _) = y_part(dy, 3)
-            (p0, n), (q0, _) = x_part(dx, 3)
-            for a in range(3):
-                send_fine(
-                    o,
-                    lambda a=a, p0=p0, n=n, q0=q0, s0=s0, sn=sn, t0=t0: (
-                        given[a].at[pl.ds(p0 - 3, n), pl.ds(s0, sn), :],
-                        mm.at[a, pl.ds(q0, n), pl.ds(t0, sn), pl.ds(0, NZ)],
-                    ),
-                )
+
+    for o in ((0, 1, 0), (0, -1, 0), (1, 1, 0), (1, -1, 0), (-1, 1, 0), (-1, -1, 0), (1, 0, 0), (-1, 0, 0)):
+        send_rows(o)
+
+    for copy in own:
+        copy.wait()
+
+    lane = iota((NY, 128), 1)
+    head = jnp.zeros((NY, 128), F32)
+    tail = jnp.zeros((NY, 128), F32)
+    for p in range(NX):
+        for a, to, depth in ((0, 0, 3), (1, 3, 2), (2, 5, 2)):
+            turned = mm[a, 3 + p, 0:NY, 0:NZ]
+            at = 8 * p + to
+            turned = pltpu.roll(turned, at, 1) if at else turned
+            head = jnp.where((lane >= at) & (lane < at + depth), turned, head)
+            behind = (lane >= at - depth) & (lane < at) if at else lane >= 128 - depth
+            tail = jnp.where(behind, turned, tail)
+    packs[0] = head
+    packs[1] = tail
+    lane8 = iota((8, 128), 1)
+    for side, pack in ((0, head), (1, tail)):
+        for e, first in ((0, 0), (1, NX - 3)):
+            small = jnp.zeros((8, 128), F32)
+            for t in range(4):
+                moved = pltpu.roll(pack[8 * t : 8 * t + 8], (32 * t - 8 * first + 8) % 128, 1)
+                small = jnp.where(lane8 // 32 == t, moved, small)
+            edges[side, e] = small
 
     def send_pack(o):
         dx, dy, dz = o
         (s0, sn), (t0, _) = y_part(dy, 3)
         side = 1 if dz == 1 else 0
-        send_fine(
-            o, lambda: (packs.at[side, pl.ds(s0, sn), :], zland.at[side, 1 - dx, pl.ds(t0, sn), :])
-        )
+        if dx and not dy:
+            send_fine(o, lambda: (edges.at[side, (dx + 1) // 2], eland.at[side, (1 - dx) // 2]))
+        else:
+            send_fine(o, lambda: (packs.at[side, pl.ds(s0, sn), :], zland.at[side, 1 - dx, pl.ds(t0, sn), :]))
 
     by_side([o for o in sorted(NEIGHBOURS, key=lambda o: o[0] != 0) if o[2] != 0], send_pack)
 
@@ -298,6 +281,9 @@
     row_ok = ((rows_in < 36) | (iy > 0)) & ((rows_in < NY) | (rows_in >= 36) | (iy < gy - 1))
     col_ok = ((lane40 < 64) & (iz < gz - 1)) | ((lane40 >= 64) & (iz > 0))
     both_ok = row_ok & col_ok
+    def turn(v, back):
+        return pltpu.roll(v, 128 - back, 1) if back else v
+
     def columns(p):
         if p < 3:
             xs, q, x_ok = 0, NX - 3 + p, ix > 0
@@ -309,17 +295,15 @@
         t = zland[1, xs]
         ok0 = row_ok if x_ok is None else row_ok & x_ok
         ok1 = both_ok if x_ok is None else both_ok & x_ok
-        g1 = jnp.where(
-            lane40 < 64, pltpu.roll(h, (-8 * q) % 128, 1), pltpu.roll(t, (-8 * q - 8) % 128, 1)
-        )
+        g1 = turn(jnp.where(lane40 % 8 < 3, h, t), 8 * q)
         mm[0, p, :, NZ:PZ] = jnp.where(ok1, g1, 0.0)
         if x_ok is None:
             mm[0, p, NY:PY, 0:NZ] = jnp.where(ok0[NY:PY], mm[0, p, NY:PY, 0:NZ], 0.0)
         else:
             mm[0, p, :, 0:NZ] = jnp.where(ok0, mm[0, p, :, 0:NZ], 0.0)
         if 0 < p < PX - 1:
-            f1 = jnp.where(lane40 < 64, pltpu.roll(h, (-8 * q - 3) % 128, 1), pltpu.roll(t, (-8 * q - 5) % 128, 1))
-            s1 = jnp.where(lane40 < 64, pltpu.roll(h, (-8 * q - 5) % 128, 1), pltpu.roll(t, (-8 * q - 3) % 128, 1))
+            f1 = turn(jnp.where((lane40 % 8 == 3) | (lane40 % 8 == 4), h, t), 8 * q + 3)
+            s1 = turn(jnp.where((lane40 % 8 == 5) | (lane40 % 8 == 6), h, t), 8 * q + 5)
             s1 = jnp.where((lane40 < 2) | (lane40 >= 126), s1, 0.0)
             mm[1, p, :, NZ:PZ] = f1
             mm[2, p, :, NZ:PZ] = s1
@@ -404,6 +388,10 @@
 
     finish([c for c in fine_copies if c[0][0] != 0], False)
 
+    for side in range(2):
+        for e, first in ((0, NX - 3), (1, 0)):
+            for t in range(4):
+                zland[side, 2 * e, 8 * t : 8 * t + 8, :] = pltpu.roll(eland[side, e], (8 * first - 8 - 32 * t) % 128, 1)
     for p in (0, 1, 2, 19, 20, 21):
         columns(p)
     outer(mm.at[0], va, (3, 2, 1, 18, 19, 20), first_sums)
@@ -535,7 +523,7 @@
     for k in (0, 2):
         pl.when(has(k - 1))(functools.partial(wait_parts, k))
 
-    lane8, row8 = iota((8, 128), 1), iota((8, 128), 0)
+    row8 = iota((8, 128), 0)
     block = (lane8 // 16) % 4
     z_ok = (block < 3) & ((block > 0) | (iz > 0)) & ((block < 2) | (iz < gz - 1))
     low = lane8 < 64
@@ -576,19 +564,24 @@
         cov[m] = coc[m] * cof[m]
 
     def coarse(i, v):
-        wrap_up = jnp.where(low, 0.0, pltpu.roll(v[15], 64, 1))
-        wrap_down = jnp.where(low, pltpu.roll(v[0], 64, 1), 0.0)
+        twice = [m + m for m in v]
+        sums = [twice[m] + pltpu.roll(v[m], 1, 1) + pltpu.roll(v[m], 127, 1) for m in range(16)]
+
+        def other_half(m):
+            u = pltpu.roll(v[m], 64, 1)
+            return u + u + pltpu.roll(v[m], 65, 1) + pltpu.roll(v[m], 63, 1)
+
+        wrap_up = jnp.where(low, 0.0, other_half(15))
+        wrap_down = jnp.where(low, other_half(0), 0.0)
         new = []
         for m in range(16):
-            up = v[m - 1] if m else wrap_up
-            down = v[m + 1] if m < 15 else wrap_down
-            a = up + down + 2.0 * v[m]
-            b = 2.0 * a + jnp.where(row8 == 0, 0.0, pltpu.roll(a, 1, 0)) + jnp.where(row8 == 7, 0.0, pltpu.roll(a, 7, 0))
-            t = 2.0 * b + pltpu.roll(b, 1, 1) + pltpu.roll(b, 127, 1)
-            new.append(0.2 * v[m] + coc[m] * (cof[m] + 0.25 * t - 2.0 * v[m]))
+            a = (sums[m - 1] if m else wrap_up) + (sums[m + 1] if m < 15 else wrap_down) + (sums[m] + sums[m])
+            b = (a + a) + jnp.where(row8 == 0, 0.0, pltpu.roll(a, 1, 0)) + jnp.where(row8 == 7, 0.0, pltpu.roll(a, 7, 0))
+            c = coc[m]
+            new.append(0.2 * v[m] + c * (cof[m] - twice[m]) + (0.25 * c) * b)
         return tuple(new)
 
-    v = lax.fori_loop(0, ITERS - 1, coarse, tuple(cov[m] for m in range(16)))
+    v = lax.fori_loop(0, ITERS - 1, coarse, tuple(cov[m] for m in range(16)), unroll=3)
     for m in range(16):
         cov[m] = v[m]
 
@@ -627,7 +620,9 @@
             vm((PX, PY, PZ), F32),
             vm((PX, PY, PZ), F32),
             vm((2, NY, 128), F32),
+            vm((2, 2, 8, 128), F32),
             vm((2, 3, PY, 128), F32),
+            vm((2, 2, 8, 128), F32),
             vm((8, NY, 128), F32),
             vm((2, 10, PY, 128), F32),
             vm((2, 10, 24, 128), F32),
@@ -653,7 +648,7 @@
             pltpu.SemaphoreType.DMA((6,)),
         ],
         compiler_params=pltpu.CompilerParams(
-            collective_id=0, has_side_effects=True, vmem_limit_bytes=60 * 1024 * 1024
+            collective_id=0, has_side_effects=True, vmem_limit_bytes=107 * 512 * 1024
         ),
         name="multigrid",
     )(guess, right_side, screen)

time: 28.3 us -> 26 us (0.919); the launches traced: 27.9 us -> 25.9 us
  Pallas kernels: 26.2 us -> 25.2 us
  local copies, waits for them, and re-layouts: 1.67 us -> 0.71 us
    pallas_call x1, Pallas kernels: 26.2 us -> 25.2 us  [on_device(): pl.pallas_call(functools.partial(kernel, sizes), out_shape=jax.ShapeDtype...]
    unnamed x1, local copies, waits for them, and re-layouts: 1.67 us -> 0.71 us
where the time goes in v3:
time: 26 us; the launch traced here: 25.9 us
  Pallas kernels  25.2 us (97%)
  local copies, waits for them, and re-layouts  0.71 us (3%)
    pallas_call x1, Pallas kernels, on_device(): pl.pallas_call(functools.partial(kernel, sizes), out_shape=jax.ShapeDtype...  25.2 us
    unnamed x1, local copies, waits for them, and re-layouts  0.71 us

profile of v3, /device:TPU:32, one launch (start us, length us, event | category | flops | bytes accessed | tf_op | source)
XLA Modules:
  0.0 25.9 jit_solution(16103058939391980748)
XLA Ops:
  0.0 25.2 %multigrid.1 = f32[16,32,128]{2,1,0:T(8,128)S(1)} custom-call(f32[16,32,128]{2,1,0:T(8,128)} %guess.1, f32[16,32,128]{2,1,0:T(8,128)} %rhs.1, f32[16,32,128]{2,1,0:T(8,128)} %scr.1), custom_call_target="tpu_custom_call" | custom-call | tf_op jit(solution)/shard_map/multigrid/pallas_call | solution.py:612
  25.2 0.7 %copy.5 = f32[16,32,128]{2,1,0:T(8,128)} copy(f32[16,32,128]{2,1,0:T(8,128)S(1)} %multigrid.1) | data formatting | bytes 524288

commit v4 on v3

--- a/solution.py
+++ b/solution.py
@@ -24,10 +24,6 @@
 
 def iota(shape, dim):
     return lax.broadcasted_iota(jnp.int32, shape, dim)
-
-
-def mod(v, n):
-    return lax.rem(v + n, n)
 
 
 def plane_sum(v):
@@ -73,6 +69,7 @@
     ms,
     mr,
     gsem,
+    ready,
 ):
     gx, gy, gz = sizes
     ix, iy, iz = lax.axis_index("gx"), lax.axis_index("gy"), lax.axis_index("gz")
@@ -96,28 +93,44 @@
 
     peers.sort(key=lambda o: -hops(o))
 
-    def has(dz):
-        return iz < gz - 1 if dz == 1 else iz > 0
-
-    def by_side(offsets, act):
-        for o in offsets:
-            if o[2] == 0:
-                act(o)
-        for dz in (1, -1):
-
-            @pl.when(has(dz))
-            def _(dz=dz):
-                for o in offsets:
-                    if o[2] == dz:
-                        act(o)
-
-    heard = [(1, 3, 0), (1, 2, 0), (1, -2, 0), (0, 3, 0), (0, 2, 0), (0, -2, 0)] + NEIGHBOURS
+    def has(axis, d):
+        at, n = ((ix, gx), (iy, gy), (iz, gz))[axis]
+        return at < n - d if d > 0 else at >= -d
+
+    def visit(items, act, sign=1):
+        def level(items, axis):
+            if axis == 3:
+                for item in items:
+                    act(item)
+                return
+            for d in sorted({item[0][axis] for item in items}, key=abs):
+                some = [item for item in items if item[0][axis] == d]
+                if d == 0:
+                    level(some, axis + 1)
+                else:
+                    pl.when(has(axis, sign * d))(functools.partial(level, some, axis + 1))
+
+        level(items, 0)
+
+    def count(axis, d):
+        return 1 + has(axis, d).astype(jnp.int32) + has(axis, -d).astype(jnp.int32)
+
+    rows_off = [(a, b, 0) for a in (0, 1, -1) for b in (2, -2)]
     barrier = pltpu.get_barrier_semaphore()
-    by_side(
-        [(-o[0], -o[1], -o[2]) for o in heard],
-        lambda o: pl.semaphore_signal(barrier, inc=1, device_id=device(o), device_id_type=MESH),
-    )
-    sides = (iz > 0).astype(jnp.int32) + (iz < gz - 1).astype(jnp.int32)
+
+    def signal(semaphore):
+        return lambda item: pl.semaphore_signal(semaphore, inc=1, device_id=device(item[0]), device_id_type=MESH)
+
+    visit([(o,) for o in NEIGHBOURS + rows_off], signal(barrier))
+    near = count(0, 1) * count(1, 1) * count(2, 1) - 1 + count(0, 1) * (count(1, 2) - 1)
+
+    told = [(a, b, 0) for a in (0, 1, -1) for b in (0, 2, -2) if a or b]
+
+    def tell(step):
+        visit([(o,) for o in told], signal(ready.at[step]))
+
+    def hear(step):
+        pl.semaphore_wait(ready.at[step], count(0, 1) * count(1, 2) - 1)
 
     own = []
     for a, ref in ((2, scr), (0, guess), (1, rhs)):
@@ -136,14 +149,40 @@
         ex[q, 17:23, :] = jnp.zeros((6, 128), F32)
     s24[...] = jnp.zeros_like(s24)
 
-    for side, dz in ((0, 1), (1, -1)):
-
-        @pl.when(jnp.logical_not(has(dz)))
-        def _(side=side, dz=dz):
-            zland[side] = jnp.zeros((3, PY, 128), F32)
-            eland[side] = jnp.zeros((2, 8, 128), F32)
-            zmid[side] = jnp.zeros((3, 24, 128), F32)
-            bf[1 + dz] = jnp.zeros((gy, gx, 8, 128), F32)
+    def blank(ref, *at):
+        ref[at] = jnp.zeros(ref.at[at].shape, F32)
+
+    whole = slice(None)
+    for e, d in ((0, -1), (1, 1)):
+
+        @pl.when(jnp.logical_not(has(0, d)))
+        def _(e=e):
+            planes = slice(3 + NX, PX) if e else slice(0, 3)
+            for a in range(3):
+                blank(mm, a, planes, whole, slice(0, NZ))
+            for side in range(2):
+                blank(zland, side, 2 * e)
+                blank(eland, side, e)
+                blank(zmid, side, 2 * e)
+            blank(ex, 9 * e)
+
+        @pl.when(jnp.logical_not(has(1, d)))
+        def _(e=e):
+            rows = slice(NY, NY + 3) if e else slice(PY - 3, PY)
+            row = slice(16, 17) if e else slice(23, 24)
+            for a in range(3):
+                blank(mm, a, whole, rows, slice(0, NZ))
+            for side in range(2):
+                blank(zland, side, whole, rows)
+                blank(zmid, side, whole, row)
+            blank(ex, whole, row)
+
+        @pl.when(jnp.logical_not(has(2, d)))
+        def _(e=e, d=d):
+            blank(zland, 1 - e)
+            blank(eland, 1 - e)
+            blank(zmid, 1 - e)
+            blank(bf, 1 + d)
 
     r_i, c_i = iota((128, 128), 0), iota((128, 128), 1)
     pool = jnp.where(r_i // 2 == c_i, 0.5, 0.0).astype(F32)
@@ -166,7 +205,11 @@
             a = a - part.astype(F32)
         return total
 
-    pl.semaphore_wait(barrier, len(heard) - 18 + 9 * sides)
+    pl.semaphore_wait(barrier, near)
+    tell(0)
+
+    for copy in own:
+        copy.wait()
 
     fine_copies = []
     given = (guess, rhs, scr)
@@ -182,24 +225,18 @@
             device_id_type=MESH,
         )
 
-    def send_fine(o, refs):
-        fine_copies.append((o, refs, (fs, fr), len(fine_copies)))
-        describe(*fine_copies[-1]).start()
+    def started(copies, sems):
+        def start(copy):
+            copies.append(copy + (sems, len(copies)))
+            describe(*copies[-1]).start()
+
+        return start
 
     def finish(copies, sending):
         def one(copy):
             describe(*copy).wait_send() if sending else describe(*copy).wait_recv()
 
-        for copy in copies:
-            if copy[0][2] == 0:
-                one(copy)
-        for dz in (1, -1):
-
-            @pl.when(has(dz if sending else -dz))
-            def _(dz=dz):
-                for copy in copies:
-                    if copy[0][2] == dz:
-                        one(copy)
+        visit(copies, one, 1 if sending else -1)
 
     def x_part(d, depth):
         if d == 0:
@@ -211,23 +248,22 @@
             return (0, NY), (0, NY)
         return ((NY - depth, depth), (PY - depth, depth)) if d == 1 else ((0, depth), (NY, depth))
 
-    def send_rows(o):
+    def rows_of(o):
+        copies = []
         for a, depth in ((0, 3), (1, 2), (2, 2)):
             (p0, n), (q0, _) = x_part(o[0], depth)
             (s0, sn), (t0, _) = y_part(o[1], depth)
-            send_fine(
-                o,
-                lambda a=a, p0=p0, n=n, q0=q0, s0=s0, sn=sn, t0=t0: (
-                    given[a].at[pl.ds(p0 - 3, n), pl.ds(s0, sn), :],
+
+            def refs(a=a, p0=p0, n=n, q0=q0, s0=s0, sn=sn, t0=t0):
+                return (
+                    mm.at[a, pl.ds(p0, n), pl.ds(s0, sn), pl.ds(0, NZ)],
                     mm.at[a, pl.ds(q0, n), pl.ds(t0, sn), pl.ds(0, NZ)],
-                ),
-            )
-
-    for o in ((0, 1, 0), (0, -1, 0), (1, 1, 0), (1, -1, 0), (-1, 1, 0), (-1, -1, 0), (1, 0, 0), (-1, 0, 0)):
-        send_rows(o)
-
-    for copy in own:
-        copy.wait()
+                )
+
+            copies.append((o, refs))
+        return copies
+
+    visit([c for o in NEIGHBOURS if o[2] == 0 for c in rows_of(o)], started(fine_copies, (fs, fr)))
 
     lane = iota((NY, 128), 1)
     head = jnp.zeros((NY, 128), F32)
@@ -251,16 +287,17 @@
                 small = jnp.where(lane8 // 32 == t, moved, small)
             edges[side, e] = small
 
-    def send_pack(o):
+    def pack_of(o):
         dx, dy, dz = o
         (s0, sn), (t0, _) = y_part(dy, 3)
         side = 1 if dz == 1 else 0
         if dx and not dy:
-            send_fine(o, lambda: (edges.at[side, (dx + 1) // 2], eland.at[side, (1 - dx) // 2]))
-        else:
-            send_fine(o, lambda: (packs.at[side, pl.ds(s0, sn), :], zland.at[side, 1 - dx, pl.ds(t0, sn), :]))
-
-    by_side([o for o in sorted(NEIGHBOURS, key=lambda o: o[0] != 0) if o[2] != 0], send_pack)
+            return o, lambda: (edges.at[side, (dx + 1) // 2], eland.at[side, (1 - dx) // 2])
+        return o, lambda: (packs.at[side, pl.ds(s0, sn), :], zland.at[side, 1 - dx, pl.ds(t0, sn), :])
+
+    visit([pack_of(o) for o in NEIGHBOURS if o[2] != 0], started(fine_copies, (fs, fr)))
+    hear(0)
+    tell(1)
 
     for q in range(8):
         rx[q] = mm[2, 3 + 2 * q, 0:NY, 0:NZ] + mm[2, 4 + 2 * q, 0:NY, 0:NZ]
@@ -275,6 +312,8 @@
         msg[k, 4:5, :] = c3 if k == 0 else pltpu.roll(c3, 16 * k, 1)
 
     finish([c for c in fine_copies if c[0][0] == 0], False)
+    hear(1)
+    tell(2)
 
     rows_in = iota((PY, 128), 0)
     lane40 = iota((PY, 128), 1)
@@ -387,6 +426,7 @@
     mid_screen(tuple(range(1, 9)))
 
     finish([c for c in fine_copies if c[0][0] != 0], False)
+    hear(2)
 
     for side in range(2):
         for e, first in ((0, NX - 3), (1, 0)):
@@ -446,7 +486,8 @@
 
     slot = bf.at[:, iy, ix, pl.ds(0, 5), :]
     def send_parts(to):
-        def one(o):
+        def one(item):
+            o = item[1]
             pltpu.make_async_remote_copy(
                 src_ref=msg.at[1 - o[2]],
                 dst_ref=slot.at[1 - o[2]],
@@ -456,7 +497,7 @@
                 device_id_type=MESH,
             ).start()
 
-        by_side(to, one)
+        visit([((0, 0, o[2]), o) for o in to], one)
 
     send_parts([o for o in peers if hops(o) > 2])
     pltpu.make_async_copy(msg.at[1], slot.at[1], gsem.at[4]).start()
@@ -468,26 +509,16 @@
     zpack[...] = ztail
     mid_copies = []
 
-    def send_mid(o):
+    def mid_of(o):
         dx, dy, dz = o
         (s0, sn), t0 = ((0, 16), 0) if dy == 0 else (((15, 1), 23) if dy == 1 else ((0, 1), 16))
         if dz == 0:
             (p0, n), q0 = ((1, 8), 1) if dx == 0 else (((8, 1), 0) if dx == 1 else ((1, 1), 9))
-
-            def refs():
-                return ex.at[pl.ds(p0, n), pl.ds(s0, sn), :], ex.at[pl.ds(q0, n), pl.ds(t0, sn), :]
-
-        else:
-            side = 1 if dz == 1 else 0
-
-            def refs():
-                return zpack.at[pl.ds(s0, sn), :], zmid.at[side, 1 - dx, pl.ds(t0, sn), :]
-
-        mid_copies.append((o, refs, (ms, mr), len(mid_copies)))
-        describe(*mid_copies[-1]).start()
-
-    by_side(NEIGHBOURS, send_mid)
-
+            return o, lambda: (ex.at[pl.ds(p0, n), pl.ds(s0, sn), :], ex.at[pl.ds(q0, n), pl.ds(t0, sn), :])
+        side = 1 if dz == 1 else 0
+        return o, lambda: (zpack.at[pl.ds(s0, sn), :], zmid.at[side, 1 - dx, pl.ds(t0, sn), :])
+
+    visit([mid_of(o) for o in NEIGHBOURS], started(mid_copies, (ms, mr)))
     send_parts([o for o in peers if hops(o) <= 2])
 
     finish(mid_copies, False)
@@ -521,7 +552,7 @@
 
     wait_parts(1)
     for k in (0, 2):
-        pl.when(has(k - 1))(functools.partial(wait_parts, k))
+        pl.when(has(2, k - 1))(functools.partial(wait_parts, k))
 
     row8 = iota((8, 128), 0)
     block = (lane8 // 16) % 4
@@ -604,7 +635,7 @@
 
     wait_sent(0)
     for dz in (1, -1):
-        pl.when(has(dz))(functools.partial(wait_sent, dz))
+        pl.when(has(2, dz))(functools.partial(wait_sent, dz))
 
 
 def on_device(sizes, guess, right_side, screen):
@@ -646,6 +677,7 @@
             pltpu.SemaphoreType.DMA((26,)),
             pltpu.SemaphoreType.DMA((26,)),
             pltpu.SemaphoreType.DMA((6,)),
+            pltpu.SemaphoreType.REGULAR((3,)),
         ],
         compiler_params=pltpu.CompilerParams(
             collective_id=0, has_side_effects=True, vmem_limit_bytes=107 * 512 * 1024

time: 26 us -> 25 us (0.962); the launches traced: 25.9 us -> 24.6 us
  Pallas kernels: 25.2 us -> 23.9 us
    pallas_call x1, Pallas kernels: 25.2 us -> 23.9 us  [on_device(): pl.pallas_call(functools.partial(kernel, sizes), out_shape=jax.ShapeDtype...]
where the time goes in v4:
time: 25 us; the launch traced here: 24.6 us
  Pallas kernels  23.9 us (96%)
  local copies, waits for them, and re-layouts  0.71 us (3%)
    pallas_call x1, Pallas kernels, on_device(): pl.pallas_call(functools.partial(kernel, sizes), out_shape=jax.ShapeDtype...  23.9 us
    unnamed x1, local copies, waits for them, and re-layouts  0.71 us

profile of v4, /device:TPU:32, one launch (start us, length us, event | category | flops | bytes accessed | tf_op | source)
XLA Modules:
  0.0 24.6 jit_solution(13928940881147471387)
XLA Ops:
  0.0 23.9 %multigrid.1 = f32[16,32,128]{2,1,0:T(8,128)S(1)} custom-call(f32[16,32,128]{2,1,0:T(8,128)} %guess.1, f32[16,32,128]{2,1,0:T(8,128)} %rhs.1, f32[16,32,128]{2,1,0:T(8,128)} %scr.1), custom_call_target="tpu_custom_call" | custom-call | tf_op jit(solution)/shard_map/multigrid/pallas_call | solution.py:643
  23.9 0.7 %copy.5 = f32[16,32,128]{2,1,0:T(8,128)} copy(f32[16,32,128]{2,1,0:T(8,128)S(1)} %multigrid.1) | data formatting | bytes 524288

commit v5 on v4

--- a/solution.py
+++ b/solution.py
@@ -24,6 +24,16 @@
 
 def iota(shape, dim):
     return lax.broadcasted_iota(jnp.int32, shape, dim)
+
+
+def row_sum(v):
+    rows = v.shape[0]
+    return v + v + pltpu.roll(v, 1, 0) + pltpu.roll(v, rows - 1, 0)
+
+
+def column_sum(v):
+    cols = v.shape[1]
+    return v + v + pltpu.roll(v, 1, 1) + pltpu.roll(v, cols - 1, 1)
 
 
 def plane_sum(v):
@@ -196,74 +206,15 @@
     gather_c = jnp.where((r_i // 4 == c_i % 16) & (r_i < 64), 0.25, 0.0).astype(F32)
 
     def dot(a, b):
-        b = b.astype(jnp.bfloat16)
-        total = None
+        parts = []
         for i in range(3):
-            part = a.astype(jnp.bfloat16)
-            term = jnp.dot(part, b, preferred_element_type=F32)
-            total = term if total is None else total + term
-            a = a - part.astype(F32)
-        return total
-
-    pl.semaphore_wait(barrier, near)
-    tell(0)
+            parts.append(a.astype(jnp.bfloat16))
+            a = a - parts[-1].astype(F32)
+        b = jnp.concatenate([b.astype(jnp.bfloat16)] * 3, axis=0)
+        return jnp.dot(jnp.concatenate(parts, axis=1), b, preferred_element_type=F32)
 
     for copy in own:
         copy.wait()
-
-    fine_copies = []
-    given = (guess, rhs, scr)
-
-    def describe(o, refs, sems, i):
-        src, dst = refs()
-        return pltpu.make_async_remote_copy(
-            src_ref=src,
-            dst_ref=dst,
-            send_sem=sems[0].at[i],
-            recv_sem=sems[1].at[i],
-            device_id=device(o),
-            device_id_type=MESH,
-        )
-
-    def started(copies, sems):
-        def start(copy):
-            copies.append(copy + (sems, len(copies)))
-            describe(*copies[-1]).start()
-
-        return start
-
-    def finish(copies, sending):
-        def one(copy):
-            describe(*copy).wait_send() if sending else describe(*copy).wait_recv()
-
-        visit(copies, one, 1 if sending else -1)
-
-    def x_part(d, depth):
-        if d == 0:
-            return (3, NX), (3, NX)
-        return ((3 + NX - depth, depth), (3 - depth, depth)) if d == 1 else ((3, depth), (3 + NX, depth))
-
-    def y_part(d, depth):
-        if d == 0:
-            return (0, NY), (0, NY)
-        return ((NY - depth, depth), (PY - depth, depth)) if d == 1 else ((0, depth), (NY, depth))
-
-    def rows_of(o):
-        copies = []
-        for a, depth in ((0, 3), (1, 2), (2, 2)):
-            (p0, n), (q0, _) = x_part(o[0], depth)
-            (s0, sn), (t0, _) = y_part(o[1], depth)
-
-            def refs(a=a, p0=p0, n=n, q0=q0, s0=s0, sn=sn, t0=t0):
-                return (
-                    mm.at[a, pl.ds(p0, n), pl.ds(s0, sn), pl.ds(0, NZ)],
-                    mm.at[a, pl.ds(q0, n), pl.ds(t0, sn), pl.ds(0, NZ)],
-                )
-
-            copies.append((o, refs))
-        return copies
-
-    visit([c for o in NEIGHBOURS if o[2] == 0 for c in rows_of(o)], started(fine_copies, (fs, fr)))
 
     lane = iota((NY, 128), 1)
     head = jnp.zeros((NY, 128), F32)
@@ -287,6 +238,63 @@
                 small = jnp.where(lane8 // 32 == t, moved, small)
             edges[side, e] = small
 
+    pl.semaphore_wait(barrier, near)
+    tell(0)
+
+    fine_copies = []
+    given = (guess, rhs, scr)
+
+    def describe(o, refs, sems, i):
+        src, dst = refs()
+        return pltpu.make_async_remote_copy(
+            src_ref=src,
+            dst_ref=dst,
+            send_sem=sems[0].at[i],
+            recv_sem=sems[1].at[i],
+            device_id=device(o),
+            device_id_type=MESH,
+        )
+
+    def started(copies, sems):
+        def start(copy):
+            copies.append(copy + (sems, len(copies)))
+            describe(*copies[-1]).start()
+
+        return start
+
+    def finish(copies, sending):
+        def one(copy):
+            describe(*copy).wait_send() if sending else describe(*copy).wait_recv()
+
+        visit(copies, one, 1 if sending else -1)
+
+    def x_part(d, depth):
+        if d == 0:
+            return (3, NX), (3, NX)
+        return ((3 + NX - depth, depth), (3 - depth, depth)) if d == 1 else ((3, depth), (3 + NX, depth))
+
+    def y_part(d, depth):
+        if d == 0:
+            return (0, NY), (0, NY)
+        return ((NY - depth, depth), (PY - depth, depth)) if d == 1 else ((0, depth), (NY, depth))
+
+    def rows_of(o):
+        copies = []
+        for a, depth in ((0, 3), (1, 2), (2, 2)):
+            (p0, n), (q0, _) = x_part(o[0], depth)
+            (s0, sn), (t0, _) = y_part(o[1], depth)
+
+            def refs(a=a, p0=p0, n=n, q0=q0, s0=s0, sn=sn, t0=t0):
+                return (
+                    mm.at[a, pl.ds(p0, n), pl.ds(s0, sn), pl.ds(0, NZ)],
+                    mm.at[a, pl.ds(q0, n), pl.ds(t0, sn), pl.ds(0, NZ)],
+                )
+
+            copies.append((o, refs))
+        return copies
+
+    visit([c for o in NEIGHBOURS if o[2] == 0 for c in rows_of(o)], started(fine_copies, (fs, fr)))
+
     def pack_of(o):
         dx, dy, dz = o
         (s0, sn), (t0, _) = y_part(dy, 3)
@@ -296,9 +304,6 @@
         return o, lambda: (packs.at[side, pl.ds(s0, sn), :], zland.at[side, 1 - dx, pl.ds(t0, sn), :])
 
     visit([pack_of(o) for o in NEIGHBOURS if o[2] != 0], started(fine_copies, (fs, fr)))
-    hear(0)
-    tell(1)
-
     for q in range(8):
         rx[q] = mm[2, 3 + 2 * q, 0:NY, 0:NZ] + mm[2, 4 + 2 * q, 0:NY, 0:NZ]
     s1_own = dot((rx[:, pl.ds(0, 16, 2), :] + rx[:, pl.ds(1, 16, 2), :]).reshape(128, 128), pool).reshape(8, 16, 128)
@@ -310,6 +315,9 @@
     c3 = OMEGA / (CENTER + jnp.sum(s4[0] + s4[1], axis=0, keepdims=True))
     for k in range(3):
         msg[k, 4:5, :] = c3 if k == 0 else pltpu.roll(c3, 16 * k, 1)
+
+    hear(0)
+    tell(1)
 
     finish([c for c in fine_copies if c[0][0] == 0], False)
     hear(1)
@@ -354,17 +362,17 @@
 
     def update(src, dst, p, b0, b1, b2):
         v = src[p]
-        t = b0 + b1 + b1 + b2
+        t = column_sum(b0 + b1 + b1 + b2)
         dst[p] = 0.2 * v + cc[p] * (mm[1, p] + 0.25 * t - 2.0 * v)
 
     def inner(src, dst, first, last):
         def body(p, carry):
             b0, b1 = carry
-            b2 = plane_sum(src[p + 1])
+            b2 = row_sum(src[p + 1])
             update(src, dst, p, b0, b1, b2)
             return b1, b2
 
-        b0, b1 = plane_sum(src[first - 1]), plane_sum(src[first])
+        b0, b1 = row_sum(src[first - 1]), row_sum(src[first])
         b2, b3 = b0, b1
         for p in range(first, last):
             b2, b3 = body(p, (b2, b3))
@@ -374,14 +382,14 @@
         for p in planes:
             for i in (p - 1, p, p + 1):
                 if i not in sums:
-                    sums[i] = plane_sum(src[i])
+                    sums[i] = row_sum(src[i])
             update(src, dst, p, sums[p - 1], sums[p], sums[p + 1])
 
     def own_sum(p):
-        return plane_sum(vb[p])[0:NY, 0:NZ]
+        return row_sum(vb[p])[0:NY]
 
     def residual(p, b0, b1, b2):
-        t = b0 + b1 + b1 + b2
+        t = column_sum(b0 + b1 + b1 + b2)[:, 0:NZ]
         v = vb[p, 0:NY, 0:NZ]
         return mm[1, p, 0:NY, 0:NZ] - (CENTER + 2.0 + mm[2, p, 0:NY, 0:NZ]) * v + 0.25 * t
 
@@ -521,30 +529,15 @@
     visit([mid_of(o) for o in NEIGHBOURS], started(mid_copies, (ms, mr)))
     send_parts([o for o in peers if hops(o) <= 2])
 
-    finish(mid_copies, False)
-    mid_sums = {}
-    for p in range(10):
-        if p == 0:
-            xs, q, x_ok = 0, 7, ix > 0
-        elif p < 9:
-            xs, q, x_ok = 1, p - 1, None
-        else:
-            xs, q, x_ok = 2, 0, ix < gx - 1
-        v = ex[p]
-        v = jnp.where(lane24 == 64, pltpu.roll(zmid[0, xs], (-q) % 128, 1), v)
-        v = jnp.where(lane24 == 127, pltpu.roll(zmid[1, xs], (127 - q) % 128, 1), v)
-        ok = ok24 if x_ok is None else ok24 & x_ok
-        mid_sums[p] = plane_sum(jnp.where(ok, v, 0.0))
-    e1 = []
-    for q in range(8):
-        t = weigh(mid_sums, q + 1)[0:16]
-        e = e_own[q][0:16]
-        e1.append(0.2 * e + c1r[q + 1, 0:16] * (f1[q] + t - 2.0 * e))
-    e1 = dot(jnp.concatenate(e1, axis=0), copy_mid).reshape(8, 16, 128)
-    e1f[:, pl.ds(0, 16, 2), :] = e1
-    e1f[:, pl.ds(1, 16, 2), :] = e1
-    for p in range(NX):
-        base[p] = vb[3 + p, 0:NY, 0:NZ] + e1f[p // 2]
+    finish(fine_copies + mid_copies, True)
+
+    def wait_sent(dz):
+        sent = dummy.at[pl.ds(0, gx * gy - (dz == 0)), pl.ds(0, 5), :]
+        pltpu.make_async_copy(sent, sent, gsem.at[1 + dz]).wait()
+
+    wait_sent(0)
+    for dz in (1, -1):
+        pl.when(has(2, dz))(functools.partial(wait_sent, dz))
 
     def wait_parts(k):
         landed = bf.at[k, :, :, pl.ds(0, 5), :]
@@ -553,6 +546,8 @@
     wait_parts(1)
     for k in (0, 2):
         pl.when(has(2, k - 1))(functools.partial(wait_parts, k))
+
+    finish(mid_copies, False)
 
     row8 = iota((8, 128), 0)
     block = (lane8 // 16) % 4
@@ -612,7 +607,33 @@
             new.append(0.2 * v[m] + c * (cof[m] - twice[m]) + (0.25 * c) * b)
         return tuple(new)
 
-    v = lax.fori_loop(0, ITERS - 1, coarse, tuple(cov[m] for m in range(16)), unroll=3)
+    mid_sums = {}
+    for p in range(10):
+        if p == 0:
+            xs, q, x_ok = 0, 7, ix > 0
+        elif p < 9:
+            xs, q, x_ok = 1, p - 1, None
+        else:
+            xs, q, x_ok = 2, 0, ix < gx - 1
+        v = ex[p]
+        v = jnp.where(lane24 == 64, pltpu.roll(zmid[0, xs], (-q) % 128, 1), v)
+        v = jnp.where(lane24 == 127, pltpu.roll(zmid[1, xs], (127 - q) % 128, 1), v)
+        ok = ok24 if x_ok is None else ok24 & x_ok
+        mid_sums[p] = plane_sum(jnp.where(ok, v, 0.0))
+    e1 = []
+    for q in range(8):
+        t = weigh(mid_sums, q + 1)[0:16]
+        e = e_own[q][0:16]
+        e1.append(0.2 * e + c1r[q + 1, 0:16] * (f1[q] + t - 2.0 * e))
+    e1 = dot(jnp.concatenate(e1, axis=0), copy_mid).reshape(8, 16, 128)
+    e1f[:, pl.ds(0, 16, 2), :] = e1
+    e1f[:, pl.ds(1, 16, 2), :] = e1
+    for p in range(NX):
+        base[p] = vb[3 + p, 0:NY, 0:NZ] + e1f[p // 2]
+
+    v = tuple(cov[m] for m in range(16))
+    for i in range(ITERS - 1):
+        v = coarse(i, v)
     for m in range(16):
         cov[m] = v[m]
 
@@ -626,16 +647,6 @@
             for p in range(8 * xc, 8 * xc + 8):
                 rows = slice(8 * t, 8 * t + 8)
                 out[p, rows, :] = base[p, rows, :] + e3
-
-    finish(fine_copies + mid_copies, True)
-
-    def wait_sent(dz):
-        sent = dummy.at[pl.ds(0, gx * gy - (dz == 0)), pl.ds(0, 5), :]
-        pltpu.make_async_copy(sent, sent, gsem.at[1 + dz]).wait()
-
-    wait_sent(0)
-    for dz in (1, -1):
-        pl.when(has(2, dz))(functools.partial(wait_sent, dz))
 
 
 def on_device(sizes, guess, right_side, screen):

time: 25 us -> 24 us (0.960)
  Pallas kernels: 23.9 us -> 22.9 us
    pallas_call x1, Pallas kernels: 23.9 us -> 22.9 us  [on_device(): pl.pallas_call(functools.partial(kernel, sizes), out_shape=jax.ShapeDtype...]
where the time goes in v5:
time: 24 us; the launch traced here: 23.7 us
  Pallas kernels  22.9 us (95%)
  local copies, waits for them, and re-layouts  0.71 us (3%)
    pallas_call x1, Pallas kernels, on_device(): pl.pallas_call(functools.partial(kernel, sizes), out_shape=jax.ShapeDtype...  22.9 us
    unnamed x1, local copies, waits for them, and re-layouts  0.71 us

profile of v5, /device:TPU:32, one launch (start us, length us, event | category | flops | bytes accessed | tf_op | source)
XLA Modules:
  0.0 23.7 jit_solution(7024552457978199566)
XLA Ops:
  0.0 22.9 %multigrid.1 = f32[16,32,128]{2,1,0:T(8,128)S(1)} custom-call(f32[16,32,128]{2,1,0:T(8,128)} %guess.1, f32[16,32,128]{2,1,0:T(8,128)} %rhs.1, f32[16,32,128]{2,1,0:T(8,128)} %scr.1), custom_call_target="tpu_custom_call" | custom-call | tf_op jit(solution)/shard_map/multigrid/pallas_call | solution.py:654
  22.9 0.7 %copy.5 = f32[16,32,128]{2,1,0:T(8,128)} copy(f32[16,32,128]{2,1,0:T(8,128)S(1)} %multigrid.1) | data formatting | bytes 524288

commit v6 on v5

--- a/solution.py
+++ b/solution.py
@@ -113,7 +113,7 @@
                 for item in items:
                     act(item)
                 return
-            for d in sorted({item[0][axis] for item in items}, key=abs):
+            for d in sorted({item[0][axis] for item in items}, key=lambda d: (abs(d), d)):
                 some = [item for item in items if item[0][axis] == d]
                 if d == 0:
                     level(some, axis + 1)
@@ -200,9 +200,11 @@
         ((r_i < 2) & (c_i == 64)) | ((r_i >= 126) & (c_i == 127)), 0.5, 0.0
     ).astype(F32)
     copy_mid = jnp.where((c_i // 2 == r_i), 1.0, 0.0).astype(F32)
-    copy_coarse = jnp.where((c_i // 8 == r_i), 1.0, 0.0).astype(F32)
+    first = jnp.where(iy < gy // 2, 16, 80)
+    copy_coarse = jnp.where((c_i // 8 + first == r_i), 1.0, 0.0).astype(F32)
     z_of = jnp.where(r_i < 64, r_i // 4 + 1, jnp.where(r_i < 68, 17, jnp.where(r_i >= 124, 0, 99)))
-    gather_f = jnp.where((c_i % 20 == z_of) & (c_i < 120), 0.25, 0.0).astype(F32)
+    c_f = (c_i + 96) % 128
+    gather_f = jnp.where((c_f % 20 == z_of) & (c_f < 120), 0.25, 0.0).astype(F32)
     gather_c = jnp.where((r_i // 4 == c_i % 16) & (r_i < 64), 0.25, 0.0).astype(F32)
 
     def dot(a, b):
@@ -239,7 +241,6 @@
             edges[side, e] = small
 
     pl.semaphore_wait(barrier, near)
-    tell(0)
 
     fine_copies = []
     given = (guess, rhs, scr)
@@ -293,7 +294,6 @@
             copies.append((o, refs))
         return copies
 
-    visit([c for o in NEIGHBOURS if o[2] == 0 for c in rows_of(o)], started(fine_copies, (fs, fr)))
 
     def pack_of(o):
         dx, dy, dz = o
@@ -304,6 +304,8 @@
         return o, lambda: (packs.at[side, pl.ds(s0, sn), :], zland.at[side, 1 - dx, pl.ds(t0, sn), :])
 
     visit([pack_of(o) for o in NEIGHBOURS if o[2] != 0], started(fine_copies, (fs, fr)))
+    visit([c for o in NEIGHBOURS if o[2] == 0 for c in rows_of(o)], started(fine_copies, (fs, fr)))
+    tell(0)
     for q in range(8):
         rx[q] = mm[2, 3 + 2 * q, 0:NY, 0:NZ] + mm[2, 4 + 2 * q, 0:NY, 0:NZ]
     s1_own = dot((rx[:, pl.ds(0, 16, 2), :] + rx[:, pl.ds(1, 16, 2), :]).reshape(128, 128), pool).reshape(8, 16, 128)
@@ -484,13 +486,14 @@
         at = (q + 4) // 4
         parts[at] = parts[at] + r if at in parts else r
     y_of = jnp.where(row24 < 16, row24 // 4 + 1, jnp.where(row24 < 18, 5, jnp.where(row24 >= 22, 0, 99)))
-    z_at = lane24 % 20
-    keep = (lane24 // 20 == y_of) & ((z_at != 0) | (iz > 0)) & ((z_at != 17) | (iz < gz - 1))
+    lane_f = (lane24 + 96) % 128
+    z_at = lane_f % 20
+    keep = (lane_f // 20 == y_of) & ((z_at != 0) | (iz > 0)) & ((z_at != 17) | (iz < gz - 1))
     stacked = dot(jnp.concatenate([parts[i] for i in range(4)], axis=0), gather_f)
     for i in range(4):
         row = jnp.sum(jnp.where(keep, stacked[24 * i : 24 * i + 24], 0.0), axis=0, keepdims=True)
         for k in range(3):
-            msg[k, i : i + 1, :] = row if k == 0 else pltpu.roll(row, 16 * k, 1)
+            msg[k, i : i + 1, :] = row if k == 2 else pltpu.roll(row, 96 + 16 * k, 1)
 
     slot = bf.at[:, iy, ix, pl.ds(0, 5), :]
     def send_parts(to):
@@ -507,7 +510,8 @@
 
         visit([((0, 0, o[2]), o) for o in to], one)
 
-    send_parts([o for o in peers if hops(o) > 2])
+    send_parts([o for o in peers if o[2] and hops(o) > 3])
+    send_parts([o for o in peers if hops(o) > 2 and not (o[2] and hops(o) > 3)])
     pltpu.make_async_copy(msg.at[1], slot.at[1], gsem.at[4]).start()
 
     ztail = jnp.zeros((16, 128), F32)
@@ -639,7 +643,6 @@
 
     mine = cov[pl.ds(4 * lax.rem(iy, 4), 4)]
     mine = mine.reshape(32, 128)
-    mine = jnp.where(iy < 4, pltpu.roll(mine, 112, 1), pltpu.roll(mine, 48, 1))
     eout[...] = dot(mine, copy_coarse).reshape(4, 8, 128)
     for xc in range(2):
         for t in range(4):

time: 24 us -> 23.6 us (0.983)
  Pallas kernels: 22.9 us -> 22.5 us
    pallas_call x1, Pallas kernels: 22.9 us -> 22.5 us  [on_device(): pl.pallas_call(functools.partial(kernel, sizes), out_shape=jax.ShapeDtype...]
where the time goes in v6:
time: 23.6 us; the launch traced here: 23.2 us
  Pallas kernels  22.5 us (95%)
  local copies, waits for them, and re-layouts  0.71 us (3%)
    pallas_call x1, Pallas kernels, on_device(): pl.pallas_call(functools.partial(kernel, sizes), out_shape=jax.ShapeDtype...  22.5 us
    unnamed x1, local copies, waits for them, and re-layouts  0.71 us

profile of v6, /device:TPU:32, one launch (start us, length us, event | category | flops | bytes accessed | tf_op | source)
XLA Modules:
  0.0 23.2 jit_solution(6014628838272436918)
XLA Ops:
  0.0 22.5 %multigrid.1 = f32[16,32,128]{2,1,0:T(8,128)S(1)} custom-call(f32[16,32,128]{2,1,0:T(8,128)} %guess.1, f32[16,32,128]{2,1,0:T(8,128)} %rhs.1, f32[16,32,128]{2,1,0:T(8,128)} %scr.1), custom_call_target="tpu_custom_call" | custom-call | tf_op jit(solution)/shard_map/multigrid/pallas_call | solution.py:657
  22.5 0.7 %copy.5 = f32[16,32,128]{2,1,0:T(8,128)} copy(f32[16,32,128]{2,1,0:T(8,128)S(1)} %multigrid.1) | data formatting | bytes 524288

commit v7 on v6

--- a/solution.py
+++ b/solution.py
@@ -107,13 +107,13 @@
         at, n = ((ix, gx), (iy, gy), (iz, gz))[axis]
         return at < n - d if d > 0 else at >= -d
 
-    def visit(items, act, sign=1):
+    def visit(items, act, sign=1, far=1):
         def level(items, axis):
             if axis == 3:
                 for item in items:
                     act(item)
                 return
-            for d in sorted({item[0][axis] for item in items}, key=lambda d: (abs(d), d)):
+            for d in sorted({item[0][axis] for item in items}, key=lambda d: (far * abs(d), d)):
                 some = [item for item in items if item[0][axis] == d]
                 if d == 0:
                     level(some, axis + 1)
@@ -131,8 +131,9 @@
     def signal(semaphore):
         return lambda item: pl.semaphore_signal(semaphore, inc=1, device_id=device(item[0]), device_id_type=MESH)
 
-    visit([(o,) for o in NEIGHBOURS + rows_off], signal(barrier))
+    visit([(o,) for o in NEIGHBOURS if 0 in o] + [(o,) for o in rows_off], signal(barrier), far=-1)
     near = count(0, 1) * count(1, 1) * count(2, 1) - 1 + count(0, 1) * (count(1, 2) - 1)
+    near = near - (count(0, 1) - 1) * (count(1, 1) - 1) * (count(2, 1) - 1)
 
     told = [(a, b, 0) for a in (0, 1, -1) for b in (0, 2, -2) if a or b]
 
@@ -303,7 +304,7 @@
             return o, lambda: (edges.at[side, (dx + 1) // 2], eland.at[side, (1 - dx) // 2])
         return o, lambda: (packs.at[side, pl.ds(s0, sn), :], zland.at[side, 1 - dx, pl.ds(t0, sn), :])
 
-    visit([pack_of(o) for o in NEIGHBOURS if o[2] != 0], started(fine_copies, (fs, fr)))
+    visit([pack_of(o) for o in NEIGHBOURS if o[2] != 0 and 0 in o], started(fine_copies, (fs, fr)))
     visit([c for o in NEIGHBOURS if o[2] == 0 for c in rows_of(o)], started(fine_copies, (fs, fr)))
     tell(0)
     for q in range(8):
@@ -318,7 +319,10 @@
     for k in range(3):
         msg[k, 4:5, :] = c3 if k == 0 else pltpu.roll(c3, 16 * k, 1)
 
+    for p in range(3, 3 + NX):
+        cc[p, 0:NY, 0:NZ] = OMEGA / (CENTER + mm[2, p, 0:NY, 0:NZ])
     hear(0)
+    visit([pack_of(o) for o in NEIGHBOURS if 0 not in o], started(fine_copies, (fs, fr)))
     tell(1)
 
     finish([c for c in fine_copies if c[0][0] == 0], False)
@@ -356,7 +360,8 @@
             s1 = jnp.where((lane40 < 2) | (lane40 >= 126), s1, 0.0)
             mm[1, p, :, NZ:PZ] = f1
             mm[2, p, :, NZ:PZ] = s1
-            cc[p, :, 0:NZ] = jnp.where(ok0, OMEGA / (CENTER + mm[2, p, :, 0:NZ]), 0.0)
+            rows = slice(0, PY) if x_ok is not None else slice(NY, PY)
+            cc[p, rows, 0:NZ] = jnp.where(ok0[rows], OMEGA / (CENTER + mm[2, p, rows, 0:NZ]), 0.0)
             cc[p, :, NZ:PZ] = jnp.where(ok1, OMEGA / (CENTER + s1), 0.0)
 
     for p in range(3, 3 + NX):

time: 23.6 us -> 23.2 us (0.983)
  Pallas kernels: 22.5 us -> 22.1 us
    pallas_call x1, Pallas kernels: 22.5 us -> 22.1 us  [on_device(): pl.pallas_call(functools.partial(kernel, sizes), out_shape=jax.ShapeDtype...]
where the time goes in v7:
time: 23.2 us; the launch traced here: 22.8 us
  Pallas kernels  22.1 us (95%)
  local copies, waits for them, and re-layouts  0.71 us (3%)
    pallas_call x1, Pallas kernels, on_device(): pl.pallas_call(functools.partial(kernel, sizes), out_shape=jax.ShapeDtype...  22.1 us
    unnamed x1, local copies, waits for them, and re-layouts  0.71 us

profile of v7, /device:TPU:32, one launch (start us, length us, event | category | flops | bytes accessed | tf_op | source)
XLA Modules:
  0.0 22.8 jit_solution(5471688655334907188)
XLA Ops:
  0.0 22.1 %multigrid.1 = f32[16,32,128]{2,1,0:T(8,128)S(1)} custom-call(f32[16,32,128]{2,1,0:T(8,128)} %guess.1, f32[16,32,128]{2,1,0:T(8,128)} %rhs.1, f32[16,32,128]{2,1,0:T(8,128)} %scr.1), custom_call_target="tpu_custom_call" | custom-call | tf_op jit(solution)/shard_map/multigrid/pallas_call | solution.py:662
  22.1 0.7 %copy.5 = f32[16,32,128]{2,1,0:T(8,128)} copy(f32[16,32,128]{2,1,0:T(8,128)S(1)} %multigrid.1) | data formatting | bytes 524288

commit v8 on v7

--- a/solution.py
+++ b/solution.py
@@ -307,6 +307,10 @@
     visit([pack_of(o) for o in NEIGHBOURS if o[2] != 0 and 0 in o], started(fine_copies, (fs, fr)))
     visit([c for o in NEIGHBOURS if o[2] == 0 for c in rows_of(o)], started(fine_copies, (fs, fr)))
     tell(0)
+    hear(0)
+    visit([pack_of(o) for o in NEIGHBOURS if 0 not in o], started(fine_copies, (fs, fr)))
+    tell(1)
+
     for q in range(8):
         rx[q] = mm[2, 3 + 2 * q, 0:NY, 0:NZ] + mm[2, 4 + 2 * q, 0:NY, 0:NZ]
     s1_own = dot((rx[:, pl.ds(0, 16, 2), :] + rx[:, pl.ds(1, 16, 2), :]).reshape(128, 128), pool).reshape(8, 16, 128)
@@ -321,9 +325,6 @@
 
     for p in range(3, 3 + NX):
         cc[p, 0:NY, 0:NZ] = OMEGA / (CENTER + mm[2, p, 0:NY, 0:NZ])
-    hear(0)
-    visit([pack_of(o) for o in NEIGHBOURS if 0 not in o], started(fine_copies, (fs, fr)))
-    tell(1)
 
     finish([c for c in fine_copies if c[0][0] == 0], False)
     hear(1)

time: 23.2 us -> 23.2 us (level)
  no operation moved by 1% of the time
where the time goes in v8:
time: 23.2 us; the launch traced here: 22.8 us
  Pallas kernels  22.1 us (95%)
  local copies, waits for them, and re-layouts  0.71 us (3%)
    pallas_call x1, Pallas kernels, on_device(): pl.pallas_call(functools.partial(kernel, sizes), out_shape=jax.ShapeDtype...  22.1 us
    unnamed x1, local copies, waits for them, and re-layouts  0.71 us

profile of v8, /device:TPU:32, one launch (start us, length us, event | category | flops | bytes accessed | tf_op | source)
XLA Modules:
  0.0 22.8 jit_solution(7083582934265274613)
XLA Ops:
  0.0 22.1 %multigrid.1 = f32[16,32,128]{2,1,0:T(8,128)S(1)} custom-call(f32[16,32,128]{2,1,0:T(8,128)} %guess.1, f32[16,32,128]{2,1,0:T(8,128)} %rhs.1, f32[16,32,128]{2,1,0:T(8,128)} %scr.1), custom_call_target="tpu_custom_call" | custom-call | tf_op jit(solution)/shard_map/multigrid/pallas_call | solution.py:663
  22.1 0.7 %copy.5 = f32[16,32,128]{2,1,0:T(8,128)} copy(f32[16,32,128]{2,1,0:T(8,128)S(1)} %multigrid.1) | data formatting | bytes 524288
